TPU v7x, 32 devices: a whole 2x2x4 slice. The times are simulated.
32 devices in a mesh: rep: 4 (over y, x), fsdp: 8 (over z, core).
Axes of the slice: x: 2, y: 2, z: 4, core: 2. Of those that a mesh axis runs over, the one named last changes fastest.
Arguments:
- tokens: bfloat16 [32768, 768], P(('rep', 'fsdp')), may hold values from -6 to 6
- lengths: int32 [4, 8], P('rep'), may hold values from 1 to 7680, 8192 in all within a row
- qkv_weight: float32 [768, 2304], P('fsdp'), may hold values from -0.21875 to 0.21875
- out_weight: float32 [768, 768], P('fsdp'), may hold values from -6 to 6
- gate_weight: float32 [768, 3072], P('fsdp'), may hold values from -0.21875 to 0.21875
- up_weight: float32 [768, 3072], P('fsdp'), may hold values from -0.21875 to 0.21875
- down_weight: float32 [3072, 768], P('fsdp'), may hold values from -0.109375 to 0.109375
- norm1_gain: float32 [768], P('fsdp'), may hold values from 0.5 to 1.5
- norm1_bias: float32 [768], P('fsdp'), may hold values from -3 to 3
- norm2_gain: float32 [768], P('fsdp'), may hold values from 0.5 to 1.5
- norm2_bias: float32 [768], P('fsdp'), may hold values from -3 to 3
- cotangent: bfloat16 [32768, 768], P(('rep', 'fsdp')), may hold values from -6 to 6
Outputs:
- layer_out: bfloat16 [32768, 768], P(('rep', 'fsdp'))
- grad_tokens: float32 [32768, 768], P(('rep', 'fsdp'))
- grad_qkv_weight: float32 [768, 2304], P('fsdp')
- grad_out_weight: float32 [768, 768], P('fsdp')
- grad_gate_weight: float32 [768, 3072], P('fsdp')
- grad_up_weight: float32 [768, 3072], P('fsdp')
- grad_down_weight: float32 [3072, 768], P('fsdp')
- grad_norm1_gain: float32 [768], P('fsdp')
- grad_norm1_bias: float32 [768], P('fsdp')
- grad_norm2_gain: float32 [768], P('fsdp')
- grad_norm2_bias: float32 [768], P('fsdp')
Inputs may be any that keep to these rules, and one draw needn't show every extreme that they name: Each row lists the lengths of 8 documents that fill one sequence in order; they sum to the sequence's tokens, and the longest covers all but 1024 // 2 of them.
All inputs are finite; a program needn't handle non-finite values.
Results may differ from a plain program's by a relative error of at most 0.018.
The roundings to bfloat16 on the way count: a program that leaves them out, or rounds other values in their place, can miss the bound.
Values may be sent and summed in bfloat16 or wider, within the bound.
No kernel may reach another device: no remote copies, remote signals or barrier semaphores. Data moves between devices by JAX's collectives and lax.ppermute only.
A program may use at most 320 MiB of HBM per device.

v0:
```python
import math

import jax
import jax.numpy as jnp
from jax import lax
from jax.sharding import PartitionSpec as P

HEADS = 12
WINDOW = 1024


epsilon = 1e-06
rope_base = 1000.0
masked_score = -1e30


def extended_2(value, sides, width):
    for axis, dim in sides:
        size, length = (lax.axis_size(axis), value.shape[dim])
        up = [(i, (i + 1) % size) for i in range(size - 1)]
        down = [(j, i) for i, j in up]
        last = lax.slice_in_dim(value, length - width, length, axis=dim)
        first = lax.slice_in_dim(value, 0, width, axis=dim)
        before = lax.ppermute(last, axis, up)
        after = lax.ppermute(first, axis, down)
        value = jnp.concatenate([before, value, after], axis=dim)
    return value


def shifted(value, axis, by):
    length = lax.axis_size(axis)
    pairs = [(i, i + by) for i in range(length) if 0 <= i + by < length]
    return lax.ppermute(value, axis, pairs)


def layout(doc_lengths, index):
    ends = jnp.cumsum(doc_lengths)
    after = (index[:, None] >= ends[None, :]).astype(jnp.int32)
    documents = jnp.sum(after, axis=1)
    starts = jnp.sum(after * doc_lengths[None, :], axis=1)
    return (documents, index - starts)


def angles(position, head_dim):
    half = head_dim // 2
    frequency = rope_base ** (-2.0 * jnp.arange(half, dtype=jnp.float32) / head_dim)
    angle = position.astype(jnp.float32)[:, None] * frequency[None, :]
    return (jnp.cos(angle)[:, None, :], jnp.sin(angle)[:, None, :])


def rotate(values, cosine, sine, heads):
    count, width = values.shape
    split = values.reshape(count, heads, width // heads)
    half = split.shape[2] // 2
    first = split[..., :half]
    second = split[..., half:]
    turned = jnp.concatenate(
        [first * cosine - second * sine, second * cosine + first * sine], axis=-1
    )
    return turned.reshape(count, width)


def unrotate(values, cosine, sine, heads):
    count, width = values.shape
    split = values.reshape(count, heads, width // heads)
    half = split.shape[2] // 2
    first = split[..., :half]
    second = split[..., half:]
    turned = jnp.concatenate(
        [first * cosine + second * sine, second * cosine - first * sine], axis=-1
    )
    return turned.reshape(count, width)


def normalize(summed, gain, shift):
    centred = summed - jnp.mean(summed, axis=-1, keepdims=True)
    inverse = lax.rsqrt(jnp.mean(centred * centred, axis=-1, keepdims=True) + epsilon)
    normed = centred * inverse
    return (normed * gain + shift, normed, inverse)


def norm_back(grad, normed, inverse, gain):
    scaled = grad * gain
    return inverse * (
        scaled
        - jnp.mean(scaled, axis=-1, keepdims=True)
        - normed * jnp.mean(scaled * normed, axis=-1, keepdims=True)
    )


def shards(
    tokens,
    lengths,
    qkv_weight,
    out_weight,
    gate_weight,
    up_weight,
    down_weight,
    norm1_gain,
    norm1_bias,
    norm2_gain,
    norm2_bias,
    cotangent,
):
    row_count, width = tokens.shape
    heads = HEADS
    head_dim = width // heads
    reach = WINDOW // 2
    block = min(512, row_count)
    blocks = row_count // block
    span = block + 2 * reach
    scale = 1.0 / math.sqrt(head_dim)
    seq_len = row_count * lax.axis_size("fsdp")
    offset = lax.axis_index("fsdp") * row_count
    doc_lengths = lengths[0]
    index = offset + jnp.arange(row_count, dtype=jnp.int32)
    documents, position = layout(doc_lengths, index)
    key_index = offset - reach + jnp.arange(row_count + 2 * reach, dtype=jnp.int32)
    key_docs, unused = layout(doc_lengths, key_index)
    key_docs = jnp.where((key_index >= 0) & (key_index < seq_len), key_docs, -1)
    cosine, sine = angles(position, head_dim)
    (
        qkv_full,
        out_full,
        gate_full,
        up_full,
        down_full,
        gain1_full,
        bias1_full,
        gain2_full,
        bias2_full,
    ) = (
        lax.all_gather(qkv_weight.astype(jnp.bfloat16), "fsdp", axis=0, tiled=True),
        lax.all_gather(out_weight.astype(jnp.bfloat16), "fsdp", axis=0, tiled=True),
        lax.all_gather(gate_weight.astype(jnp.bfloat16), "fsdp", axis=0, tiled=True),
        lax.all_gather(up_weight.astype(jnp.bfloat16), "fsdp", axis=0, tiled=True),
        lax.all_gather(down_weight.astype(jnp.bfloat16), "fsdp", axis=0, tiled=True),
        lax.all_gather(norm1_gain.astype(jnp.bfloat16), "fsdp", axis=0, tiled=True),
        lax.all_gather(norm1_bias.astype(jnp.bfloat16), "fsdp", axis=0, tiled=True),
        lax.all_gather(norm2_gain.astype(jnp.bfloat16), "fsdp", axis=0, tiled=True),
        lax.all_gather(norm2_bias.astype(jnp.bfloat16), "fsdp", axis=0, tiled=True),
    )
    joint = jnp.dot(tokens, qkv_full, preferred_element_type=jnp.float32)
    queries = rotate(joint[:, :width], cosine, sine, heads).astype(jnp.bfloat16)
    keys = rotate(joint[:, width : 2 * width], cosine, sine, heads).astype(jnp.bfloat16)
    values = joint[:, 2 * width :].astype(jnp.bfloat16)
    extended = extended_2(jnp.concatenate([keys, values], axis=1), (("fsdp", 0),), reach)
    key_ext = extended[:, :width].reshape(row_count + 2 * reach, heads, head_dim)
    value_ext = extended[:, width:].reshape(row_count + 2 * reach, heads, head_dim)
    query_heads = queries.reshape(row_count, heads, head_dim)

    def block_scores(start):
        query_rows = lax.dynamic_slice_in_dim(query_heads, start, block, 0)
        key_rows = lax.dynamic_slice_in_dim(key_ext, start, span, 0)
        value_rows = lax.dynamic_slice_in_dim(value_ext, start, span, 0)
        query_place = lax.dynamic_slice_in_dim(index, start, block, 0)
        key_place = lax.dynamic_slice_in_dim(key_index, start, span, 0)
        query_docs = lax.dynamic_slice_in_dim(documents, start, block, 0)
        near_docs = lax.dynamic_slice_in_dim(key_docs, start, span, 0)
        near = (query_docs[:, None] == near_docs[None, :]) & (
            jnp.abs(query_place[:, None] - key_place[None, :]) <= reach
        )
        scores = (
            jnp.einsum("qhd,khd->hqk", query_rows, key_rows, preferred_element_type=jnp.float32)
            * scale
        )
        return (query_rows, key_rows, value_rows, jnp.where(near[None], scores, masked_score))

    def forward_block(number):
        start = number * block
        query_rows, key_rows, value_rows, scores = block_scores(start)
        peak = jnp.max(scores, axis=-1, keepdims=True)
        raised = jnp.exp(scores - peak)
        total = jnp.sum(raised, axis=-1, keepdims=True)
        weights = (raised / total).astype(jnp.bfloat16)
        mixed = jnp.einsum("hqk,khd->qhd", weights, value_rows, preferred_element_type=jnp.float32)
        return (mixed, peak[..., 0] + jnp.log(total[..., 0]))

    mixed, logsum = lax.map(forward_block, jnp.arange(blocks, dtype=jnp.int32))
    attended = mixed.reshape(row_count, width).astype(jnp.bfloat16)
    branch = jnp.dot(attended, out_full, preferred_element_type=jnp.float32)
    hidden, normed1, inverse1 = normalize(
        tokens.astype(jnp.float32) + branch,
        gain1_full.astype(jnp.float32),
        bias1_full.astype(jnp.float32),
    )
    hidden_low = hidden.astype(jnp.bfloat16)
    gate = jnp.dot(hidden_low, gate_full, preferred_element_type=jnp.float32)
    lift = jnp.dot(hidden_low, up_full, preferred_element_type=jnp.float32)
    sigma = jax.nn.sigmoid(gate)
    product = (gate * sigma * lift).astype(jnp.bfloat16)
    feed = jnp.dot(product, down_full, preferred_element_type=jnp.float32)
    result, normed2, inverse2 = normalize(
        hidden + feed, gain2_full.astype(jnp.float32), bias2_full.astype(jnp.float32)
    )
    (
        qkv_back,
        out_back,
        gate_back,
        up_back,
        down_back,
        gain1_back,
        bias1_back,
        gain2_back,
        bias2_back,
    ) = (
        lax.all_gather(qkv_weight.astype(jnp.bfloat16), "fsdp", axis=0, tiled=True),
        lax.all_gather(out_weight.astype(jnp.bfloat16), "fsdp", axis=0, tiled=True),
        lax.all_gather(gate_weight.astype(jnp.bfloat16), "fsdp", axis=0, tiled=True),
        lax.all_gather(up_weight.astype(jnp.bfloat16), "fsdp", axis=0, tiled=True),
        lax.all_gather(down_weight.astype(jnp.bfloat16), "fsdp", axis=0, tiled=True),
        lax.all_gather(norm1_gain.astype(jnp.bfloat16), "fsdp", axis=0, tiled=True),
        lax.all_gather(norm1_bias.astype(jnp.bfloat16), "fsdp", axis=0, tiled=True),
        lax.all_gather(norm2_gain.astype(jnp.bfloat16), "fsdp", axis=0, tiled=True),
        lax.all_gather(norm2_bias.astype(jnp.bfloat16), "fsdp", axis=0, tiled=True),
    )
    grad_result = cotangent.astype(jnp.float32)
    grad_gain2 = jnp.sum(grad_result * normed2, axis=0)
    grad_bias2 = jnp.sum(grad_result, axis=0)
    grad_sum2 = norm_back(grad_result, normed2, inverse2, gain2_back.astype(jnp.float32))
    grad_feed = grad_sum2.astype(jnp.bfloat16)
    grad_down = jnp.einsum("tf,td->fd", product, grad_feed, preferred_element_type=jnp.float32)
    grad_product = jnp.einsum("td,fd->tf", grad_feed, down_back, preferred_element_type=jnp.float32)
    grad_gate = (grad_product * lift * sigma * (1.0 + gate * (1.0 - sigma))).astype(jnp.bfloat16)
    grad_lift = (grad_product * gate * sigma).astype(jnp.bfloat16)
    grad_gate_w = jnp.einsum("td,tf->df", hidden_low, grad_gate, preferred_element_type=jnp.float32)
    grad_up_w = jnp.einsum("td,tf->df", hidden_low, grad_lift, preferred_element_type=jnp.float32)
    grad_hidden = grad_sum2 + jnp.einsum(
        "tf,df->td", grad_gate, gate_back, preferred_element_type=jnp.float32
    )
    grad_hidden = grad_hidden + jnp.einsum(
        "tf,df->td", grad_lift, up_back, preferred_element_type=jnp.float32
    )
    grad_gain1 = jnp.sum(grad_hidden * normed1, axis=0)
    grad_bias1 = jnp.sum(grad_hidden, axis=0)
    grad_sum1 = norm_back(grad_hidden, normed1, inverse1, gain1_back.astype(jnp.float32))
    grad_branch = grad_sum1.astype(jnp.bfloat16)
    grad_out_w = jnp.einsum("td,te->de", attended, grad_branch, preferred_element_type=jnp.float32)
    grad_attended = jnp.einsum(
        "te,de->td", grad_branch, out_back, preferred_element_type=jnp.float32
    )
    grad_heads = grad_attended.astype(jnp.bfloat16).reshape(row_count, heads, head_dim)

    def backward_block(carry, number):
        grad_keys, grad_values = carry
        start = number * block
        query_rows, key_rows, value_rows, scores = block_scores(start)
        chance = jnp.exp(scores - logsum[number][..., None])
        grad_rows = lax.dynamic_slice_in_dim(grad_heads, start, block, 0)
        grad_chance = jnp.einsum(
            "qhd,khd->hqk", grad_rows, value_rows, preferred_element_type=jnp.float32
        )
        centre = jnp.sum(chance * grad_chance, axis=-1, keepdims=True)
        grad_scores = (chance * (grad_chance - centre)).astype(jnp.bfloat16)
        grad_query = (
            jnp.einsum("hqk,khd->qhd", grad_scores, key_rows, preferred_element_type=jnp.float32)
            * scale
        )
        key_part = (
            jnp.einsum("hqk,qhd->khd", grad_scores, query_rows, preferred_element_type=jnp.float32)
            * scale
        )
        value_part = jnp.einsum(
            "hqk,qhd->khd",
            chance.astype(jnp.bfloat16),
            grad_rows,
            preferred_element_type=jnp.float32,
        )
        grad_keys = lax.dynamic_update_slice_in_dim(
            grad_keys, lax.dynamic_slice_in_dim(grad_keys, start, span, 0) + key_part, start, 0
        )
        grad_values = lax.dynamic_update_slice_in_dim(
            grad_values,
            lax.dynamic_slice_in_dim(grad_values, start, span, 0) + value_part,
            start,
            0,
        )
        return ((grad_keys, grad_values), grad_query)

    zeros = jnp.zeros((row_count + 2 * reach, heads, head_dim), jnp.float32)
    (grad_keys, grad_values), grad_query = lax.scan(
        backward_block, (zeros, zeros), jnp.arange(blocks, dtype=jnp.int32)
    )
    grad_pairs = jnp.concatenate(
        [
            grad_keys.reshape(row_count + 2 * reach, width),
            grad_values.reshape(row_count + 2 * reach, width),
        ],
        axis=1,
    )
    from_next = shifted(grad_pairs[:reach].astype(jnp.bfloat16), "fsdp", -1).astype(jnp.float32)
    from_prior = shifted(grad_pairs[row_count + reach :].astype(jnp.bfloat16), "fsdp", 1).astype(
        jnp.float32
    )
    owned = grad_pairs[reach : reach + row_count]
    owned = owned.at[:reach].add(from_prior)
    owned = owned.at[row_count - reach :].add(from_next)
    grad_q = unrotate(grad_query.reshape(row_count, width), cosine, sine, heads)
    grad_k = unrotate(owned[:, :width], cosine, sine, heads)
    grad_joint = jnp.concatenate([grad_q, grad_k, owned[:, width:]], axis=1).astype(jnp.bfloat16)
    grad_qkv_w = jnp.einsum("td,te->de", tokens, grad_joint, preferred_element_type=jnp.float32)
    grad_inputs = grad_sum1 + jnp.einsum(
        "te,de->td", grad_joint, qkv_back, preferred_element_type=jnp.float32
    )
    (
        share_qkv,
        share_out,
        share_gate,
        share_up,
        share_down,
        share_gain1,
        share_bias1,
        share_gain2,
        share_bias2,
    ) = (
        lax.psum_scatter(grad_qkv_w, "fsdp", scatter_dimension=0, tiled=True),
        lax.psum_scatter(grad_out_w, "fsdp", scatter_dimension=0, tiled=True),
        lax.psum_scatter(grad_gate_w, "fsdp", scatter_dimension=0, tiled=True),
        lax.psum_scatter(grad_up_w, "fsdp", scatter_dimension=0, tiled=True),
        lax.psum_scatter(grad_down, "fsdp", scatter_dimension=0, tiled=True),
        lax.psum_scatter(grad_gain1, "fsdp", scatter_dimension=0, tiled=True),
        lax.psum_scatter(grad_bias1, "fsdp", scatter_dimension=0, tiled=True),
        lax.psum_scatter(grad_gain2, "fsdp", scatter_dimension=0, tiled=True),
        lax.psum_scatter(grad_bias2, "fsdp", scatter_dimension=0, tiled=True),
    )
    summed = lax.psum(
        (
            share_qkv,
            share_out,
            share_gate,
            share_up,
            share_down,
            share_gain1,
            share_bias1,
            share_gain2,
            share_bias2,
        ),
        "rep",
    )
    return (
        result.astype(jnp.bfloat16),
        grad_inputs,
        summed[0],
        summed[1],
        summed[2],
        summed[3],
        summed[4],
        summed[5],
        summed[6],
        summed[7],
        summed[8],
    )


def solution(mesh):
    return jax.shard_map(
        shards,
        mesh=mesh,
        in_specs=(
            P(("rep", "fsdp"), None),
            P("rep", None),
            P("fsdp", None),
            P("fsdp", None),
            P("fsdp", None),
            P("fsdp", None),
            P("fsdp", None),
            P("fsdp"),
            P("fsdp"),
            P("fsdp"),
            P("fsdp"),
            P(("rep", "fsdp"), None),
        ),
        out_specs=(
            P(("rep", "fsdp"), None),
            P(("rep", "fsdp"), None),
            P("fsdp", None),
            P("fsdp", None),
            P("fsdp", None),
            P("fsdp", None),
            P("fsdp", None),
            P("fsdp"),
            P("fsdp"),
            P("fsdp"),
            P("fsdp"),
        ),
        check_vma=False,
    )
```

profile of v0, /device:TPU:0, one launch (start us, length us, event | category | flops | bytes accessed | tf_op | source)
XLA Modules:
  0.0 1329.1 jit_solution(5791599703860090403)
XLA Ops:
  17.1 37.4 %all-gather.6.cloned.1.call-done = bf16[768,2304]{1,0:T(8,128)(2,1)} async-done(((bf16[96,2304]{1,0:T(8,128)(2,1)}), bf16[768,2304]{1,0:T(8,128)(2,1)}) %all-gather.6.cloned.1.call-update) | async-done | bytes 3538960 | tf_op jit(solution)/shard_map/all_gather | solution.py:133
  54.5 5.8 fusion.79
  91.4 59.2 %all-reduce.11 = (bf16[768]{0:T(1024)(128)(2,1)S(1)}, bf16[768]{0:T(1024)(128)(2,1)S(1)}, bf16[768]{0:T(1024)(128)(2,1)S(1)}, bf16[768]{0:T(1024)(128)(2,1)S(1)}) all-reduce(bf16[768]{0:T(1024)(128)(2,1)S(1)} %dynamic-update-slice.7, bf16[768]{0:T(1024)(128)(2,1)S(1)} %dynamic-update-slice.6, ...), channel_id=1, replica_groups=mesh['rep'=4,'fsdp'=8] {'fsdp'}, use_global_device_ids=true, to_apply=%add.1 | all-reduce | flops 3072 | bytes 12288
  171.8 115.1 %while.28 = (s32[]{:T(128)}, bf16[2,512,12,64]{1,3,2,0:T(8,128)(2,1)}, f32[2,12,512]{2,1,0:T(8,128)}, s32[2]{0:T(128)S(1)}, bf16[2048,12,64]{0,2,1:T(8,128)(2,1)...) while((s32[]{:T(128)}, ...), condition=%wide.region_7.8_spmd, body=%wide.region_4.7_spmd.sunk | while | flops 2533091328 | bytes 136324400 | solution.py:179
  177.3 17.1 %fusion.128 = (f32[12,512]{1,0:T(8,128)S(1)}, f32[12,512,1536]{2,1,0:T(8,128)}) fusion(pred[512,1536]{1,0:T(8,128)(4,1)S(1)} %fusion.127, bf16[2048,12,64]{0,2,1:T(8,128)(2,1)S(1)} %get-tuple-element.560, s32[]{:T(128)S(6)} %select_n.79, bf16[1024,12,64]{0,2,1:T(8,128)(2,1)} %get-tuple-element.559, s32[]{:T(128)S(6)} %select_n.80), kind=kOutput, calls=%fused_computation.3.clone.1 | convolution fusion | flops 1236264960 | bytes 41705480 | tf_op jit(solution)/shard_map/while/body/eval_jaxpr/qhd,khd->hqk/dot_general | solution.py:164
  194.4 17.7 %fusion.129 = f32[12,512]{1,0:T(8,128)S(1)} fusion(f32[12,512,1536]{2,1,0:T(8,128)} %get-tuple-element.500, f32[12,512]{1,0:T(8,128)S(1)} %get-tuple-element.501, pred[512,1536]{1,0:T(8,128)(4,1)S(1)} %fusion.127), kind=kLoop, calls=%fused_computation.4.clone.1 | loop fusion | flops 37742592 | bytes 38584320 | tf_op jit(solution)/shard_map/while/body/eval_jaxpr/reduce_sum | solution.py:174
  212.8 16.7 %bitcast_dynamic-update-slice_fusion.4 = bf16[2,512,12,64]{1,3,2,0:T(8,128)(2,1)} fusion(bf16[2,512,12,64]{1,3,2,0:T(8,128)(2,1)} %get-tuple-element.535, s32[]{:T(128)} %get-tuple-element.534, f32[12,512,1536]{2,1,0:T(8,128)} %get-tuple-element.500, f32[12,512]{1,0:T(8,128)S(1)} %fusion.129, f32[12,512]{1,0:T(8,128)S(1)} %get-tuple-element.501, ...), kind=kOutput, calls=%fused_computation.11.clone.1 | convolution fusion | flops 1255145472 | bytes 42533380 | tf_op jit(solution)/shard_map/while/body/eval_jaxpr/hqk,khd->qhd/dot_general | solution.py:176
  234.8 17.2 %fusion.128 = (f32[12,512]{1,0:T(8,128)S(1)}, f32[12,512,1536]{2,1,0:T(8,128)}) fusion(pred[512,1536]{1,0:T(8,128)(4,1)S(1)} %fusion.127, bf16[2048,12,64]{0,2,1:T(8,128)(2,1)S(1)} %get-tuple-element.560, s32[]{:T(128)S(6)} %select_n.79, bf16[1024,12,64]{0,2,1:T(8,128)(2,1)} %get-tuple-element.559, s32[]{:T(128)S(6)} %select_n.80), kind=kOutput, calls=%fused_computation.3.clone.1 | convolution fusion | flops 1236264960 | bytes 41705480 | tf_op jit(solution)/shard_map/while/body/eval_jaxpr/qhd,khd->hqk/dot_general | solution.py:164
  252.0 17.4 %fusion.129 = f32[12,512]{1,0:T(8,128)S(1)} fusion(f32[12,512,1536]{2,1,0:T(8,128)} %get-tuple-element.500, f32[12,512]{1,0:T(8,128)S(1)} %get-tuple-element.501, pred[512,1536]{1,0:T(8,128)(4,1)S(1)} %fusion.127), kind=kLoop, calls=%fused_computation.4.clone.1 | loop fusion | flops 37742592 | bytes 38584320 | tf_op jit(solution)/shard_map/while/body/eval_jaxpr/reduce_sum | solution.py:174
  270.1 16.4 %bitcast_dynamic-update-slice_fusion.4 = bf16[2,512,12,64]{1,3,2,0:T(8,128)(2,1)} fusion(bf16[2,512,12,64]{1,3,2,0:T(8,128)(2,1)} %get-tuple-element.535, s32[]{:T(128)} %get-tuple-element.534, f32[12,512,1536]{2,1,0:T(8,128)} %get-tuple-element.500, f32[12,512]{1,0:T(8,128)S(1)} %fusion.129, f32[12,512]{1,0:T(8,128)S(1)} %get-tuple-element.501, ...), kind=kOutput, calls=%fused_computation.11.clone.1 | convolution fusion | flops 1255145472 | bytes 42533380 | tf_op jit(solution)/shard_map/while/body/eval_jaxpr/hqk,khd->qhd/dot_general | solution.py:176
  298.7 10.2 fusion.80
  308.9 14.5 %multiply_convert_fusion.3 = (bf16[1024,3072]{1,0:T(8,128)(2,1)}, f32[1024,3072]{1,0:T(8,128)}) fusion(f32[1024,3072]{1,0:T(8,128)} %fusion.80, bf16[1024,768]{0,1:T(8,128)(2,1)} %fusion.56, bf16[768,3072]{1,0:T(8,128)(2,1)} %all-gather.12.cloned.1.call-done), kind=kOutput, calls=%fused_computation.57 | convolution fusion | flops 4850712576 | bytes 37748736 | tf_op jit(solution)/shard_map/dot_general | solution.py:189
  323.4 9.6 fusion.78
  338.9 21.2 %multiply_convert_fusion.1 = (bf16[1024,3072]{1,0:T(8,128)(2,1)}, bf16[1024,3072]{1,0:T(8,128)(2,1)}) fusion(f32[1024,3072]{1,0:T(8,128)} %fusion.80, f32[1024,3072]{1,0:T(8,128)} %get-tuple-element.352, bf16[3072,768]{1,0:T(8,128)(2,1)} %all-gather.14.cloned.1.call-done, f32[1024]{0:T(1024)S(1)} %get-tuple-element.356, f32[1024,768]{0,1:T(8,128)} %copy-done.4, ...), kind=kOutput, calls=%fused_computation.55 | convolution fusion | flops 4879810560 | bytes 47205376 | tf_op jit(solution)/shard_map/td,fd->tf/dot_general | solution.py:223
  360.2 8.7 fusion.81
  369.0 9.5 multiply_reduce_fusion.1
  389.2 326.3 %while.29 = (s32[]{:T(128)}, f32[2048,12,64]{0,2,1:T(8,128)}, f32[2048,12,64]{0,2,1:T(8,128)}, f32[2,512,12,64]{1,0,3,2:T(2,128)}, s32[2]{0:T(128)S(1)}, /*index...) while((s32[]{:T(128)}, f32[2048,12,64]{0,2,1:T(8,128)}, ...), condition=%wide.region_18.19_spmd, body=%wide.region_16.18_spmd.sunk | while | flops 6189213696 | bytes 326590816 | solution.py:281
  390.9 16.0 %fusion.138 = f32[12,512,1536]{2,1,0:T(8,128)} fusion(bf16[2048,12,64]{0,2,1:T(8,128)(2,1)S(1)} %get-tuple-element.616, s32[]{:T(128)S(6)} %select_n.84, bf16[1024,12,64]{0,2,1:T(8,128)(2,1)} %get-tuple-element.611, s32[]{:T(128)S(6)} %select_n.85), kind=kOutput, calls=%fused_computation.34.clone.1 | convolution fusion | flops 1207959552 | bytes 40894472 | tf_op jit(solution)/shard_map/while/body/eval_jaxpr/qhd,khd->hqk/dot_general | solution.py:164
  414.6 30.7 %multiply_reduce_fusion.7 = (f32[12,512]{1,0:T(8,128)S(1)}, f32[12,512,1536]{2,1,0:T(8,128)}) fusion(f32[12,512,1536]{2,1,0:T(8,128)} %fusion.138, f32[12,512]{1,0:T(8,128)S(1)} %dynamic-slice_bitcast_fusion.2, pred[512,1536]{1,0:T(8,128)(4,1)} %fusion.139, bf16[2048,12,64]{0,2,1:T(8,128)(2,1)} %get-tuple-element.619, s32[]{:T(128)S(6)} %select_n.84, ...), kind=kOutput, calls=%fused_computation.19.clone.1 | convolution fusion | flops 1255139328 | bytes 79478792 | tf_op jit(solution)/shard_map/while/body/eval_jaxpr/qhd,khd->hqk/dot_general | solution.py:250
  445.3 31.6 %multiply_convert_fusion.5 = bf16[12,512,1536]{2,1,0:T(8,128)(2,1)} fusion(f32[12,512,1536]{2,1,0:T(8,128)} %get-tuple-element.516, f32[12,512,1536]{2,1,0:T(8,128)} %fusion.138, f32[12,512]{1,0:T(8,128)S(1)} %get-tuple-element.517, f32[12,512]{1,0:T(8,128)S(1)} %dynamic-slice_bitcast_fusion.2, pred[512,1536]{1,0:T(8,128)(4,1)S(1)} %copy-done), kind=kLoop, calls=%fused_computation.18.clone.1 | loop fusion | flops 56623104 | bytes 95207424 | tf_op jit(solution)/shard_map/while/body/eval_jaxpr/convert_element_type | solution.py:254
  476.9 9.6 multiply_bitcast_fusion.2
  489.2 28.9 %dynamic_update_slice.30 = f32[2,512,12,64]{1,0,3,2:T(2,128)} dynamic-update-slice(f32[2,512,12,64]{1,0,3,2:T(2,128)} %get-tuple-element.589, f32[1,512,12,64]{1,0,3,2:T(1,128)} %copy.106, s32[]{:T(128)} %get-tuple-element.586, s32[]{:T(128)} %constant.140.clone.1..sunk.1, s32[]{:T(128)} %constant.140.clone.1..sunk.1, s32[]{:T(128)} %constant.140.clone.1..sunk.1) | dynamic-update-slice | bytes 3145732 | tf_op jit(solution)/shard_map/while/body/jit(dynamic_update_index_in_dim)/dynamic_update_slice | solution.py:179
  518.1 13.3 %fusion.140 = f32[2048,12,64]{0,2,1:T(8,128)} fusion(f32[2048,12,64]{0,2,1:T(8,128)} %get-tuple-element.587, s32[]{:T(128)S(6)} %select_n.84, bf16[12,512,1536]{2,1,0:T(8,128)(2,1)} %multiply_convert_fusion.5, bf16[1024,12,64]{0,2,1:T(8,128)(2,1)} %get-tuple-element.611, s32[]{:T(128)S(6)} %select_n.85), kind=kOutput, calls=%fused_computation.27.clone.1 | convolution fusion | flops 1210318848 | bytes 29097992 | tf_op jit(solution)/shard_map/while/body/eval_jaxpr/hqk,qhd->khd/dot_general | solution.py:260
  531.5 21.1 %fusion.141 = f32[2048,12,64]{0,2,1:T(8,128)} fusion(f32[2048,12,64]{0,2,1:T(8,128)} %get-tuple-element.588, s32[]{:T(128)S(6)} %select_n.84, f32[12,512,1536]{2,1,0:T(8,128)} %fusion.138, f32[12,512]{1,0:T(8,128)S(1)} %dynamic-slice_bitcast_fusion.2, pred[512,1536]{1,0:T(8,128)(4,1)} %fusion.139, bf16[1024,12,64]{0,2,1:T(8,128)(2,1)} %get-tuple-element.618, ...), kind=kOutput, calls=%fused_computation.25.clone.1 | convolution fusion | flops 1246887936 | bytes 48783368 | tf_op jit(solution)/shard_map/while/body/eval_jaxpr/hqk,qhd->khd/dot_general | solution.py:263
  553.8 16.0 %fusion.138 = f32[12,512,1536]{2,1,0:T(8,128)} fusion(bf16[2048,12,64]{0,2,1:T(8,128)(2,1)S(1)} %get-tuple-element.616, s32[]{:T(128)S(6)} %select_n.84, bf16[1024,12,64]{0,2,1:T(8,128)(2,1)} %get-tuple-element.611, s32[]{:T(128)S(6)} %select_n.85), kind=kOutput, calls=%fused_computation.34.clone.1 | convolution fusion | flops 1207959552 | bytes 40894472 | tf_op jit(solution)/shard_map/while/body/eval_jaxpr/qhd,khd->hqk/dot_general | solution.py:164
  577.5 30.6 %multiply_reduce_fusion.7 = (f32[12,512]{1,0:T(8,128)S(1)}, f32[12,512,1536]{2,1,0:T(8,128)}) fusion(f32[12,512,1536]{2,1,0:T(8,128)} %fusion.138, f32[12,512]{1,0:T(8,128)S(1)} %dynamic-slice_bitcast_fusion.2, pred[512,1536]{1,0:T(8,128)(4,1)} %fusion.139, bf16[2048,12,64]{0,2,1:T(8,128)(2,1)} %get-tuple-element.619, s32[]{:T(128)S(6)} %select_n.84, ...), kind=kOutput, calls=%fused_computation.19.clone.1 | convolution fusion | flops 1255139328 | bytes 79478792 | tf_op jit(solution)/shard_map/while/body/eval_jaxpr/qhd,khd->hqk/dot_general | solution.py:250
  608.1 31.6 %multiply_convert_fusion.5 = bf16[12,512,1536]{2,1,0:T(8,128)(2,1)} fusion(f32[12,512,1536]{2,1,0:T(8,128)} %get-tuple-element.516, f32[12,512,1536]{2,1,0:T(8,128)} %fusion.138, f32[12,512]{1,0:T(8,128)S(1)} %get-tuple-element.517, f32[12,512]{1,0:T(8,128)S(1)} %dynamic-slice_bitcast_fusion.2, pred[512,1536]{1,0:T(8,128)(4,1)S(1)} %copy-done), kind=kLoop, calls=%fused_computation.18.clone.1 | loop fusion | flops 56623104 | bytes 95207424 | tf_op jit(solution)/shard_map/while/body/eval_jaxpr/convert_element_type | solution.py:254
  639.7 9.6 multiply_bitcast_fusion.2
  652.1 28.9 %dynamic_update_slice.30 = f32[2,512,12,64]{1,0,3,2:T(2,128)} dynamic-update-slice(f32[2,512,12,64]{1,0,3,2:T(2,128)} %get-tuple-element.589, f32[1,512,12,64]{1,0,3,2:T(1,128)} %copy.106, s32[]{:T(128)} %get-tuple-element.586, s32[]{:T(128)} %constant.140.clone.1..sunk.1, s32[]{:T(128)} %constant.140.clone.1..sunk.1, s32[]{:T(128)} %constant.140.clone.1..sunk.1) | dynamic-update-slice | bytes 3145732 | tf_op jit(solution)/shard_map/while/body/jit(dynamic_update_index_in_dim)/dynamic_update_slice | solution.py:179
  681.0 13.3 %fusion.140 = f32[2048,12,64]{0,2,1:T(8,128)} fusion(f32[2048,12,64]{0,2,1:T(8,128)} %get-tuple-element.587, s32[]{:T(128)S(6)} %select_n.84, bf16[12,512,1536]{2,1,0:T(8,128)(2,1)} %multiply_convert_fusion.5, bf16[1024,12,64]{0,2,1:T(8,128)(2,1)} %get-tuple-element.611, s32[]{:T(128)S(6)} %select_n.85), kind=kOutput, calls=%fused_computation.27.clone.1 | convolution fusion | flops 1210318848 | bytes 29097992 | tf_op jit(solution)/shard_map/while/body/eval_jaxpr/hqk,qhd->khd/dot_general | solution.py:260
  694.3 21.0 %fusion.141 = f32[2048,12,64]{0,2,1:T(8,128)} fusion(f32[2048,12,64]{0,2,1:T(8,128)} %get-tuple-element.588, s32[]{:T(128)S(6)} %select_n.84, f32[12,512,1536]{2,1,0:T(8,128)} %fusion.138, f32[12,512]{1,0:T(8,128)S(1)} %dynamic-slice_bitcast_fusion.2, pred[512,1536]{1,0:T(8,128)(4,1)} %fusion.139, bf16[1024,12,64]{0,2,1:T(8,128)(2,1)} %get-tuple-element.618, ...), kind=kOutput, calls=%fused_computation.25.clone.1 | convolution fusion | flops 1246887936 | bytes 48783368 | tf_op jit(solution)/shard_map/while/body/eval_jaxpr/hqk,qhd->khd/dot_general | solution.py:263
  715.5 8.2 fusion.42
  731.3 5.8 reshape_reshape.3
  751.8 9.2 convolution_bitcast_fusion
  761.0 8.1 copy.88
  769.2 5.4 fusion.60
  774.7 10.7 fusion.63
  786.8 10.1 fusion.82
  797.0 10.2 fusion.83
  807.4 46.6 %reduce-scatter.16.cloned.1.call-done = f32[96,2304]{1,0:T(8,128)} async-done(((f32[768,2304]{1,0:T(8,128)}), f32[96,2304]{1,0:T(8,128)}) %reduce-scatter.16.cloned.1.call-update) | async-done | bytes 884752
  856.6 34.4 %reduce-scatter.8.cloned.1.call-done = f32[96,768]{1,0:T(8,128)} async-done(((f32[768,768]{1,0:T(8,128)}), f32[96,768]{1,0:T(8,128)}) %reduce-scatter.8.cloned.1.call-update) | async-done | bytes 294928 | tf_op jit(solution)/shard_map/reduce_scatter | solution.py:317
  890.9 101.1 %reduce-scatter.14.cloned.1.call-done = f32[384,768]{1,0:T(8,128)} async-done(((f32[3072,768]{1,0:T(8,128)}), f32[384,768]{1,0:T(8,128)}) %reduce-scatter.14.cloned.1.call-update) | async-done | bytes 1179664 | tf_op jit(solution)/shard_map/reduce_scatter | solution.py:320
  992.1 100.2 %reduce-scatter.10.cloned.1.call-done = f32[96,3072]{1,0:T(8,128)} async-done(((f32[768,3072]{1,0:T(8,128)}), f32[96,3072]{1,0:T(8,128)}) %reduce-scatter.10.cloned.1.call-update) | async-done | bytes 1179664 | tf_op jit(solution)/shard_map/reduce_scatter | solution.py:318
  1092.3 100.0 %reduce-scatter.12.cloned.1.call-done = f32[96,3072]{1,0:T(8,128)} async-done(((f32[768,3072]{1,0:T(8,128)}), f32[96,3072]{1,0:T(8,128)}) %reduce-scatter.12.cloned.1.call-update) | async-done | bytes 1179664 | tf_op jit(solution)/shard_map/reduce_scatter | solution.py:319
  1193.0 25.9 %all-reduce.8 = (f32[768]{0:T(1024)S(1)}, f32[768]{0:T(1024)S(1)}, f32[768]{0:T(1024)S(1)}, f32[768]{0:T(1024)S(1)}) all-reduce(f32[768]{0:T(1024)S(1)} %copy-done.38, f32[768]{0:T(1024)S(1)} %copy-done.39, f32[768]{0:T(1024)S(1)} %copy-done.36, f32[768]{0:T(1024)S(1)} %copy-done.37), channel_id=7, replica_groups=mesh['rep'=4,'fsdp'=8] {'fsdp'}, use_global_device_ids=true, to_apply=%region_30.31.clone | all-reduce | flops 3072 | bytes 24576
  1220.8 10.6 all-reduce.9
  1231.4 8.3 fusion.58
  1242.1 72.8 %all-reduce.14.cloned.1.call-done = (f32[96,2304]{0,1:T(8,128)}, f32[96,768]{1,0:T(8,128)}, f32[96,3072]{1,0:T(8,128)}, f32[96,3072]{1,0:T(8,128)}, f32[384,768]{1,0:T(8,128)}) async-done(((f32[96,2304]{0,1:T(8,128)}, f32[96,768]{1,0:T(8,128)}, f32[96,3072]{1,0:T(8,128)}, f32[96,3072]{1,0:T(8,128)}, f32[384,768]{1,0:T(8,128)}), (f32[96,2304]{0,1:T(8,128)}, f32[96,768]{1,0:T(8,128)}, f32[96,3072]{1,0:T(8,128)}, ...) | async-done | bytes 4718608 | tf_op jit(solution)/shard_map/psum | solution.py:326
  (267 shorter events, 157.0 us)
Async XLA Ops:
  7.2 47.3 %all-gather.6.cloned.1.call-start = ((), (), s32[]{:S(2)}) async-start(), calls=%async_computation.5 | async-start | bytes 3981312 | tf_op jit(solution)/shard_map/all_gather | solution.py:133
  9.3 45.2 %copy-start.13 = (bf16[1024,768]{1,0:T(8,128)(2,1)S(1)}, bf16[1024,768]{1,0:T(8,128)(2,1)}, u32[]{:S(2)}) copy-start(bf16[1024,768]{1,0:T(8,128)(2,1)} %param.20) | copy-start | bytes 4718596
  9.3 282.3 %all-gather.8.cloned.1.call-start = ((), (), s32[]{:S(2)}) async-start(), calls=%async_computation.6 | async-start | bytes 1327104 | tf_op jit(solution)/shard_map/all_gather | solution.py:134
  11.1 287.6 %all-gather.10.cloned.1.call-start = ((), (), s32[]{:S(2)}) async-start(), calls=%async_computation.7 | async-start | bytes 5308416 | tf_op jit(solution)/shard_map/all_gather | solution.py:135
  12.1 296.8 %all-gather.12.cloned.1.call-start = ((), (), s32[]{:S(2)}) async-start(), calls=%async_computation.8 | async-start | bytes 5308416 | tf_op jit(solution)/shard_map/all_gather | solution.py:136
  14.3 309.0 %all-gather.14.cloned.1.call-start = ((), (), s32[]{:S(2)}) async-start(), calls=%async_computation.9 | async-start | bytes 5308416 | tf_op jit(solution)/shard_map/all_gather | solution.py:137
  17.1 53.6 %copy-start.18 = (f32[1024,32]{0,1:T(8,128)}, f32[1024,32]{0,1:T(8,128)S(1)}, u32[]{:S(2)}) copy-start(f32[1024,32]{0,1:T(8,128)S(1)} %get-tuple-element.345) | copy-start | bytes 393220
  17.1 53.6 %copy-start.20 = (f32[1024,32]{0,1:T(8,128)}, f32[1024,32]{0,1:T(8,128)S(1)}, u32[]{:S(2)}) copy-start(f32[1024,32]{0,1:T(8,128)S(1)} %get-tuple-element.346) | copy-start | bytes 393220
  78.8 6.7 copy-start.23
  80.7 8.5 copy-start.47
  80.7 8.5 copy-start.48
  80.7 8.5 copy-start.49
  80.7 8.5 copy-start.50
  80.7 8.5 copy-start.44
  80.8 79.4 %collective-permute-start = (bf16[512,1536]{1,0:T(8,128)(2,1)}, bf16[512,1536]{1,0:T(8,128)(2,1)}, u32[]{:S(2)}, u32[]{:S(2)}) collective-permute-start(bf16[512,1536]{1,0:T(8,128)(2,1)} %get-tuple-element.339), channel_id=1, source_target_pairs={{0,1},{1,2},{2,3},{3,4},{4,5},{5,6},{6,7},{8,9},{9,10},{10,11},{11... | collective-permute-start | bytes 4718600 | tf_op jit(solution)/shard_map/ppermute | solution.py:24
  84.2 76.0 %collective-permute-start.1 = (bf16[512,1536]{1,0:T(8,128)(2,1)}, bf16[512,1536]{1,0:T(8,128)(2,1)}, u32[]{:S(2)}, u32[]{:S(2)}) collective-permute-start(bf16[512,1536]{1,0:T(8,128)(2,1)} %get-tuple-element.340), channel_id=1, source_target_pairs={{1,0},{2,1},{3,2},{4,3},{5,4},{6,5},{7,6},{9,8},{10,9},{11,10},{12... | collective-permute-start | bytes 4718600 | tf_op jit(solution)/shard_map/ppermute | solution.py:25
  86.5 767.5 %reduce-scatter.16.cloned.1.call-start = ((), (), s32[]{:S(2)}) async-start(), calls=%async_computation.14 | async-start | bytes 7962624
  194.4 18.4 %copy-start.1 = (bf16[2048,12,64]{0,2,1:T(8,128)(2,1)S(1)}, bf16[2048,12,64]{0,2,1:T(8,128)(2,1)}, u32[]{:S(2)}) copy-start(bf16[2048,12,64]{0,2,1:T(8,128)(2,1)} %get-tuple-element.554) | copy-start | bytes 9437188 | tf_op jit(solution)/shard_map/while
  252.0 18.0 %copy-start.1 = (bf16[2048,12,64]{0,2,1:T(8,128)(2,1)S(1)}, bf16[2048,12,64]{0,2,1:T(8,128)(2,1)}, u32[]{:S(2)}) copy-start(bf16[2048,12,64]{0,2,1:T(8,128)(2,1)} %get-tuple-element.554) | copy-start | bytes 9437188 | tf_op jit(solution)/shard_map/while
  333.0 6.0 copy-start.4
  333.0 35.9 %copy-start.27 = (f32[1024]{0:T(1024)}, f32[1024]{0:T(1024)S(1)}, u32[]{:S(2)}) copy-start(f32[1024]{0:T(1024)S(1)} %broadcast_multiply_fusion.4) | copy-start | bytes 12292
  335.5 33.4 %copy-start.32 = (f32[1024]{0:T(1024)}, f32[1024]{0:T(1024)S(1)}, u32[]{:S(2)}) copy-start(f32[1024]{0:T(1024)S(1)} %add_rsqrt_fusion) | copy-start | bytes 12292
  338.9 30.0 %copy-start.40 = (f32[1024]{0:T(1024)}, f32[1024]{0:T(1024)S(1)}, u32[]{:S(2)}) copy-start(f32[1024]{0:T(1024)S(1)} %get-tuple-element.356) | copy-start | bytes 12292
  338.9 30.0 %copy-start.42 = (f32[1024]{0:T(1024)}, f32[1024]{0:T(1024)S(1)}, u32[]{:S(2)}) copy-start(f32[1024]{0:T(1024)S(1)} %get-tuple-element.357) | copy-start | bytes 12292
  360.2 8.8 copy-start.3
  360.2 8.8 copy-start.5
  360.2 8.8 copy-start.10
  360.2 8.8 copy-start.51
  414.6 30.7 %copy-start = (pred[512,1536]{1,0:T(8,128)(4,1)S(1)}, pred[512,1536]{1,0:T(8,128)(4,1)}, u32[]{:S(2)}) copy-start(pred[512,1536]{1,0:T(8,128)(4,1)} %fusion.139) | copy-start | bytes 2359300 | tf_op jit(solution)/shard_map/while
  577.5 30.6 %copy-start = (pred[512,1536]{1,0:T(8,128)(4,1)S(1)}, pred[512,1536]{1,0:T(8,128)(4,1)}, u32[]{:S(2)}) copy-start(pred[512,1536]{1,0:T(8,128)(4,1)} %fusion.139) | copy-start | bytes 2359300 | tf_op jit(solution)/shard_map/while
  727.6 13.1 collective-permute-start.2
  730.0 13.6 %collective-permute-start.3 = (bf16[512,1536]{0,1:T(8,128)(2,1)}, bf16[512,1536]{0,1:T(8,128)(2,1)}, u32[]{:S(2)}, u32[]{:S(2)}) collective-permute-start(bf16[512,1536]{0,1:T(8,128)(2,1)} %get-tuple-element.326), channel_id=1, source_target_pairs={{1,0},{2,1},{3,2},{4,3},{5,4},{6,5},{7,6},{9,8},{10,9},{11,10},{12... | collective-permute-start | bytes 4718600 | tf_op jit(solution)/shard_map/ppermute | solution.py:33
  731.3 9.4 slice-start
  769.1 5.6 copy-start.6
  769.1 5.6 copy-start.28
  769.1 5.6 copy-start.31
  769.1 5.6 copy-start.33
  769.2 5.6 copy-start.41
  769.2 121.7 %reduce-scatter.8.cloned.1.call-start = ((), (), s32[]{:S(2)}) async-start(), calls=%async_computation.10 | async-start | bytes 2654208 | tf_op jit(solution)/shard_map/reduce_scatter | solution.py:317
  774.6 217.4 %reduce-scatter.14.cloned.1.call-start = ((), (), s32[]{:S(2)}) async-start(), calls=%async_computation.13 | async-start | bytes 10616832 | tf_op jit(solution)/shard_map/reduce_scatter | solution.py:320
  785.4 306.8 %reduce-scatter.10.cloned.1.call-start = ((), (), s32[]{:S(2)}) async-start(), calls=%async_computation.11 | async-start | bytes 10616832 | tf_op jit(solution)/shard_map/reduce_scatter | solution.py:318
  797.0 395.4 %reduce-scatter.12.cloned.1.call-start = ((), (), s32[]{:S(2)}) async-start(), calls=%async_computation.12 | async-start | bytes 10616832 | tf_op jit(solution)/shard_map/reduce_scatter | solution.py:319
  807.3 385.7 %copy-start.36 = (f32[768]{0:T(1024)S(1)}, f32[768]{0:T(1024)}, u32[]{:S(2)}) copy-start(f32[768]{0:T(1024)} %get-tuple-element.243) | copy-start | bytes 9220
  807.3 385.7 %copy-start.37 = (f32[768]{0:T(1024)S(1)}, f32[768]{0:T(1024)}, u32[]{:S(2)}) copy-start(f32[768]{0:T(1024)} %get-tuple-element.248) | copy-start | bytes 9220
  807.3 385.7 %copy-start.38 = (f32[768]{0:T(1024)S(1)}, f32[768]{0:T(1024)}, u32[]{:S(2)}) copy-start(f32[768]{0:T(1024)} %get-tuple-element.241) | copy-start | bytes 9220
  807.3 385.7 %copy-start.39 = (f32[768]{0:T(1024)S(1)}, f32[768]{0:T(1024)}, u32[]{:S(2)}) copy-start(f32[768]{0:T(1024)} %get-tuple-element.246) | copy-start | bytes 9220
  807.3 412.0 %copy-start.11 = (bf16[1024,768]{0,1:T(8,128)(2,1)S(1)}, bf16[1024,768]{0,1:T(8,128)(2,1)}, u32[]{:S(2)}) copy-start(bf16[1024,768]{0,1:T(8,128)(2,1)} %get-tuple-element.338) | copy-start | bytes 4718596
  807.3 507.5 %all-reduce.14.cloned.1.call-start = ((), (), s32[]{:S(2)}) async-start(), calls=%async_computation.15 | async-start | bytes 10027008 | tf_op jit(solution)/shard_map/psum | solution.py:326
  (23 other events, 63.2 us)
Sparse Core Ops, SparseCore 0:
  10.2 44.2 all-gather.5
  56.7 21.5 all-gather.7
  80.5 59.5 all-gather.9
  142.1 56.2 all-gather.11
  200.0 50.5 all-gather.13
  769.2 84.7 reduce-scatter.15
  856.3 34.5 reduce-scatter.7
  893.2 98.7 reduce-scatter.13
  994.4 97.8 reduce-scatter.9
  1094.4 97.8 reduce-scatter.11
  1197.2 117.5 all-reduce.13
where the time goes:
time: 1340 us; the launch traced here: 1330 us
  waiting for transfers between devices  493 us (37%)
  matrix products  388 us (29%)
  local copies, waits for them, and re-layouts  160 us (12%)
  other arithmetic  159 us (12%)
  blocking collectives  95.7 us (7%)
  between operations  16.2 us (1%)
    reduce_scatter x1, waiting for transfers between devices, shards(): lax.psum_scatter(grad_down, 'fsdp', scatter_dimension=0, tiled=True)  101 us
    reduce_scatter x1, waiting for transfers between devices, shards(): lax.psum_scatter(grad_gate_w, 'fsdp', scatter_dimension=0, tiled=True)  100 us
    reduce_scatter x1, waiting for transfers between devices, shards(): lax.psum_scatter(grad_up_w, 'fsdp', scatter_dimension=0, tiled=True)  100 us
    unnamed x2, blocking collectives  85.1 us
    psum x1, waiting for transfers between devices, shards(): lax.psum((share_qkv, share_out, share_gate, share_up, share_down, share_g...  72.8 us
    dot_general x4, matrix products, block_scores(): jnp.einsum('qhd,khd->hqk', query_rows, key_rows, preferred_element_type=j...  66.3 us
    dynamic_update_slice x4, local copies, waits for them, and re-layouts, shards(): mixed, logsum = lax.map(forward_block, jnp.arange(blocks, dtype=jnp.int32))  63.3 us
    convert_element_type x2, other arithmetic, backward_block(): grad_scores = (chance * (grad_chance - centre)).astype(jnp.bfloat16)  63.2 us
  transfers between devices with their start and end apart: 15, of which 7 were waited for; matrix products, arithmetic and copies ran while one was open for 20% of the time, Pallas kernels for 0%

commit v1 on v0

v1 whole, which is shorter than its diff:
```python
import functools
import math

import jax
import jax.numpy as jnp
from jax import lax
from jax.experimental import pallas as pl
from jax.experimental.pallas import tpu as pltpu
from jax.sharding import PartitionSpec as P

HEADS = 12
WINDOW = 1024
REACH = WINDOW // 2
HEAD = 64
PAIR = 2 * HEAD
QUERY_BLOCK = 256
TOKEN_BLOCK = 256
VMEM = 56 * 1024 * 1024

epsilon = 1e-06
rope_base = 1000.0
masked_score = -1e30
low = jnp.bfloat16
full = jnp.float32


def dot_nn(a, b):
    return lax.dot_general(a, b, (((1,), (0,)), ((), ())), preferred_element_type=full)


def dot_nt(a, b):
    return lax.dot_general(a, b, (((1,), (1,)), ((), ())), preferred_element_type=full)


def dot_tn(a, b):
    return lax.dot_general(a, b, (((0,), (0,)), ((), ())), preferred_element_type=full)


def params():
    return pltpu.CompilerParams(vmem_limit_bytes=VMEM)


def shape(dims, dtype):
    return jax.ShapeDtypeStruct(dims, dtype)


def tables(position):
    lane = jnp.arange(PAIR, dtype=jnp.int32) % HEAD
    half = HEAD // 2
    frequency = rope_base ** (-2.0 * (lane % half).astype(full) / HEAD)
    angle = position.astype(full)[:, None] * frequency[None, :]
    sign = jnp.where(lane < half, -1.0, 1.0).astype(full)
    return jnp.cos(angle), jnp.sin(angle) * sign[None, :]


def partner(x):
    half = HEAD // 2
    lane = lax.broadcasted_iota(jnp.int32, x.shape, 1) % HEAD
    return jnp.where(lane < half, pltpu.roll(x, PAIR - half, 1), pltpu.roll(x, half, 1))


def turn(x, cosine, sine):
    return x * cosine + partner(x) * sine


def turn_back(x, cosine, sine):
    return x * cosine - partner(x) * sine


def project_kernel(plan, sources, first, count, ids, tok_ref, cos_ref, sin_ref, *refs):
    srcs = refs[:sources]
    q_ref, k_ref, v_ref, weight, sems = refs[sources:]
    step = pl.program_id(0)
    copies = plan(ids, srcs, weight, sems)

    @pl.when(step == 0)
    def _():
        for copy in copies:
            copy.start()
        for copy in copies:
            copy.wait()

    width = tok_ref.shape[1]
    rows = tok_ref[...]
    cosine = cos_ref[...]
    sine = sin_ref[...]
    keys = dot_nn(rows, weight[1])
    for at in range(0, width, PAIR):
        k_ref[:, at : at + PAIR] = turn(keys[:, at : at + PAIR], cosine, sine).astype(low)
    v_ref[...] = dot_nn(rows, weight[2]).astype(low)

    @pl.when((step >= first) & (step < first + count))
    def _():
        queries = dot_nn(rows, weight[0])
        for at in range(0, width, PAIR):
            turned = turn(queries[:, at : at + PAIR], cosine, sine).astype(low)
            q_ref[:, at : at + PAIR] = (turned.astype(full) * (1.0 / math.sqrt(HEAD))).astype(low)


def project(plan, ids, tokens, cosine, sine, sources, rows):
    ext, width = tokens.shape
    block = TOKEN_BLOCK
    first, count = (ext - rows) // 2 // block, rows // block
    tile = lambda w: pl.BlockSpec((block, w), lambda i, *_: (i, 0))
    inner = pl.BlockSpec((block, width), lambda i, *_: (jnp.clip(i - first, 0, count - 1), 0))
    return pl.pallas_call(
        functools.partial(project_kernel, plan, len(sources), first, count),
        grid_spec=pltpu.PrefetchScalarGridSpec(
            num_scalar_prefetch=1,
            grid=(ext // block,),
            in_specs=[tile(width), tile(PAIR), tile(PAIR)]
            + [pl.BlockSpec(memory_space=pl.ANY)] * len(sources),
            out_specs=[inner, tile(width), tile(width)],
            scratch_shapes=[
                pltpu.VMEM((3, width, width), low),
                pltpu.SemaphoreType.DMA((1,)),
            ],
        ),
        out_shape=[shape((rows, width), low), shape((ext, width), low), shape((ext, width), low)],
        compiler_params=params(),
        cost_estimate=pl.CostEstimate(
            flops=2 * width * width * (2 * ext + rows),
            bytes_accessed=12 * ext * width,
            transcendentals=0,
        ),
        name="project",
    )(ids, tokens, cosine, sine, *sources)


def fill_bias(bounds_ref, bias_ref, blocks, span):
    for b in range(blocks):
        lo = bounds_ref[0:1, b * QUERY_BLOCK : (b + 1) * QUERY_BLOCK] - b * QUERY_BLOCK
        hi = bounds_ref[1:2, b * QUERY_BLOCK : (b + 1) * QUERY_BLOCK] - b * QUERY_BLOCK
        at = lax.broadcasted_iota(jnp.int32, (span, QUERY_BLOCK), 0)
        bias_ref[b] = jnp.where((at >= lo) & (at < hi), 0.0, masked_score)


def only(x, head):
    lane = lax.broadcasted_iota(jnp.int32, x.shape, 1)
    return jnp.where((lane >= HEAD) if head else (lane < HEAD), x, jnp.zeros_like(x))


def attend_kernel(chunk, bounds_ref, q_ref, k_ref, v_ref, o_ref, lse_ref, bias_ref, vt_ref, s_ref):
    rows = q_ref.shape[0]
    block = QUERY_BLOCK
    blocks = rows // block
    span = k_ref.shape[0] - rows + block

    @pl.when(pl.program_id(0) == 0)
    def _():
        fill_bias(bounds_ref, bias_ref, blocks, span)

    vt_ref[...] = v_ref[...].T
    chunks = [(c, min(chunk, span - c)) for c in range(0, span, chunk)]
    for b in range(blocks):
        out = []
        for h in range(2):
            query = only(q_ref[b * block : (b + 1) * block, :], h)
            slot = s_ref.at[(2 * b + h) % 2]
            top = None
            for c, n in chunks:
                s = dot_nt(k_ref[b * block + c : b * block + c + n, :], query)
                s = s + bias_ref[b, c : c + n, :]
                slot[c : c + n, :] = s
                t = jnp.max(s.reshape(n // 8, 8, block), axis=0)
                top = t if top is None else jnp.maximum(top, t)
            peak = jnp.max(top, axis=0, keepdims=True)
            total = None
            mixed = None
            for c, n in chunks:
                e = jnp.exp(slot[c : c + n, :] - peak)
                t = jnp.sum(e.reshape(n // 8, 8, block), axis=0)
                total = t if total is None else total + t
                o = dot_nn(
                    vt_ref[h * HEAD : (h + 1) * HEAD, b * block + c : b * block + c + n],
                    e.astype(low),
                )
                mixed = o if mixed is None else mixed + o
            total = jnp.sum(total, axis=0, keepdims=True)
            out.append(mixed / total)
            lse_ref[0, h : h + 1, b * block : (b + 1) * block] = peak + jnp.log(total)
        o_ref[b * block : (b + 1) * block, :] = jnp.concatenate(out, axis=0).T.astype(low)


def attend(bounds, q, k, v, chunk=640):
    rows, width = q.shape
    ext = k.shape[0]
    pairs = width // PAIR
    blocks = rows // QUERY_BLOCK
    span = ext - rows + QUERY_BLOCK
    own = pl.BlockSpec((rows, PAIR), lambda p: (0, p))
    wide = pl.BlockSpec((ext, PAIR), lambda p: (0, p))
    return pl.pallas_call(
        functools.partial(attend_kernel, chunk),
        grid=(pairs,),
        in_specs=[pl.BlockSpec((2, rows), lambda p: (0, 0)), own, wide, wide],
        out_specs=[own, pl.BlockSpec((1, 2, rows), lambda p: (p, 0, 0))],
        out_shape=[shape((rows, width), low), shape((pairs, 2, rows), full)],
        scratch_shapes=[
            pltpu.VMEM((blocks, span, QUERY_BLOCK), full),
            pltpu.VMEM((PAIR, ext), low),
            pltpu.VMEM((2, span, QUERY_BLOCK), full),
        ],
        compiler_params=params(),
        cost_estimate=pl.CostEstimate(
            flops=16 * rows * span * width,
            bytes_accessed=4 * ext * width,
            transcendentals=rows * span * width // HEAD,
        ),
        name="attend",
    )(bounds, q, k, v)


def attend_back_kernel(
    chunk,
    bounds_ref,
    q_ref,
    k_ref,
    v_ref,
    o_ref,
    do_ref,
    lse_ref,
    dq_ref,
    own_ref,
    prior_ref,
    next_ref,
    bias_ref,
    kt_ref,
    dk_ref,
    dv_ref,
):
    rows = q_ref.shape[0]
    ext = k_ref.shape[0]
    block = QUERY_BLOCK
    blocks = rows // block
    reach = (ext - rows) // 2
    span = ext - rows + block

    @pl.when(pl.program_id(0) == 0)
    def _():
        fill_bias(bounds_ref, bias_ref, blocks, span)

    kt_ref[...] = k_ref[...].T
    dk_ref[...] = jnp.zeros_like(dk_ref)
    dv_ref[...] = jnp.zeros_like(dv_ref)
    chunks = [(c, min(chunk, span - c)) for c in range(0, span, chunk)]
    for b in range(blocks):
        at = slice(b * block, (b + 1) * block)
        q = q_ref[at, :]
        do = do_ref[at, :]
        product = (do.astype(full) * o_ref[at, :].astype(full)).T
        query = [only(q, h) for h in range(2)]
        grad = [only(do, h) for h in range(2)]
        delta = [
            jnp.sum(product[h * HEAD : (h + 1) * HEAD], axis=0, keepdims=True) for h in range(2)
        ]
        lse = [lse_ref[0, h : h + 1, at] for h in range(2)]
        dq = [None, None]
        queries = jnp.concatenate(query, axis=0)
        grads = jnp.concatenate(grad, axis=0)
        for c, n in chunks:
            lo = b * block + c
            keys = k_ref[lo : lo + n, :]
            values = v_ref[lo : lo + n, :]
            chances = []
            grad_scores = []
            for h in range(2):
                s = dot_nt(keys, query[h]) + bias_ref[b, c : c + n, :]
                p = jnp.exp(s - lse[h])
                dp = dot_nt(values, grad[h])
                ds = (p * (dp - delta[h])).astype(low)
                chances.append(p.astype(low))
                grad_scores.append(ds)
                t = dot_nn(kt_ref[h * HEAD : (h + 1) * HEAD, lo : lo + n], ds)
                dq[h] = t if dq[h] is None else dq[h] + t
            dv_ref[lo : lo + n, :] += dot_nn(jnp.concatenate(chances, axis=1), grads)
            dk_ref[lo : lo + n, :] += dot_nn(jnp.concatenate(grad_scores, axis=1), queries)
        dq_ref[at, :] = jnp.concatenate(dq, axis=0).T * (1.0 / math.sqrt(HEAD))
    for i, ref in enumerate((dk_ref, dv_ref)):
        prior_ref[i] = ref[:reach, :].astype(low)
        own_ref[i] = ref[reach : reach + rows, :]
        next_ref[i] = ref[reach + rows :, :].astype(low)


def attend_back(bounds, q, k, v, o, do, lse, chunk=1280):
    rows, width = q.shape
    ext = k.shape[0]
    pairs = width // PAIR
    blocks = rows // QUERY_BLOCK
    reach = (ext - rows) // 2
    span = ext - rows + QUERY_BLOCK
    own = pl.BlockSpec((rows, PAIR), lambda p: (0, p))
    wide = pl.BlockSpec((ext, PAIR), lambda p: (0, p))
    both = lambda n: pl.BlockSpec((2, n, PAIR), lambda p: (0, 0, p))
    return pl.pallas_call(
        functools.partial(attend_back_kernel, chunk),
        grid=(pairs,),
        in_specs=[
            pl.BlockSpec((2, rows), lambda p: (0, 0)),
            own,
            wide,
            wide,
            own,
            own,
            pl.BlockSpec((1, 2, rows), lambda p: (p, 0, 0)),
        ],
        out_specs=[own, both(rows), both(reach), both(reach)],
        out_shape=[
            shape((rows, width), full),
            shape((2, rows, width), full),
            shape((2, reach, width), low),
            shape((2, reach, width), low),
        ],
        scratch_shapes=[
            pltpu.VMEM((blocks, span, QUERY_BLOCK), full),
            pltpu.VMEM((PAIR, ext), low),
            pltpu.VMEM((ext, PAIR), full),
            pltpu.VMEM((ext, PAIR), full),
        ],
        compiler_params=params(),
        cost_estimate=pl.CostEstimate(
            flops=40 * rows * span * width,
            bytes_accessed=20 * rows * width,
            transcendentals=rows * span * width // HEAD,
        ),
        name="attend_back",
    )(bounds, q, k, v, o, do, lse)


def mean(x):
    return jnp.mean(x, axis=-1, keepdims=True)


def norm(x):
    centred = x - mean(x)
    inverse = lax.rsqrt(mean(centred * centred) + epsilon)
    return centred * inverse, inverse


def norm_back(scaled, normed, inverse):
    return inverse * (scaled - mean(scaled) - normed * mean(scaled * normed))


def middle_kernel(plan, sources, ids, at_ref, tok_ref, cot_ref, vec_ref, *refs):
    srcs = refs[:sources]
    (
        out_ref,
        dz1_ref,
        da_ref,
        hidden_ref,
        product_ref,
        dfeed_ref,
        dgate_ref,
        dlift_ref,
        dbranch_ref,
        gains_ref,
        out_w,
        gate_w,
        up_w,
        down_w,
        lift_factor,
        gate_factor,
        sems,
    ) = refs[sources:]
    step = pl.program_id(0)
    copies = plan(ids, srcs, (out_w, gate_w, up_w, down_w), sems)

    @pl.when(step == 0)
    def _():
        for group in copies:
            for copy in group:
                copy.start()
        gains_ref[...] = jnp.zeros_like(gains_ref)

    def ready(*groups):
        @pl.when(step == 0)
        def _():
            for group in groups:
                for copy in copies[group]:
                    copy.wait()

    parts, _, width = gate_w.shape
    gain1, bias1, gain2, bias2 = (vec_ref[i : i + 1] for i in range(4))
    ready(0)
    normed1, inverse1 = norm(tok_ref[...].astype(full) + dot_nn(at_ref[...], out_w[...]))
    hidden = normed1 * gain1 + bias1
    hidden_low = hidden.astype(low)
    hidden_ref[...] = hidden_low
    ready(1, 2, 3)
    feed = None
    for part in range(parts):
        at = slice(part * width, (part + 1) * width)
        gate = dot_nn(hidden_low, gate_w[part])
        lift = dot_nn(hidden_low, up_w[part])
        sigma = jax.nn.sigmoid(gate)
        opened = gate * sigma
        product = (opened * lift).astype(low)
        product_ref[:, at] = product
        lift_factor[:, at] = opened
        gate_factor[:, at] = lift * sigma * (1.0 + gate * (1.0 - sigma))
        term = dot_nn(product, down_w[at, :])
        feed = term if feed is None else feed + term
    normed2, inverse2 = norm(hidden + feed)
    out_ref[...] = (normed2 * gain2 + bias2).astype(low)
    cot = cot_ref[...].astype(full)
    gains_ref[2:3] += jnp.sum(cot * normed2, axis=0, keepdims=True)
    gains_ref[3:4] += jnp.sum(cot, axis=0, keepdims=True)
    grad = norm_back(cot * gain2, normed2, inverse2)
    dfeed = grad.astype(low)
    dfeed_ref[...] = dfeed
    for part in range(parts):
        at = slice(part * width, (part + 1) * width)
        dproduct = dot_nt(dfeed, down_w[at, :])
        dgate = (dproduct * gate_factor[:, at]).astype(low)
        dlift = (dproduct * lift_factor[:, at]).astype(low)
        dgate_ref[:, at] = dgate
        dlift_ref[:, at] = dlift
        grad = grad + dot_nt(dgate, gate_w[part]) + dot_nt(dlift, up_w[part])
    gains_ref[0:1] += jnp.sum(grad * normed1, axis=0, keepdims=True)
    gains_ref[1:2] += jnp.sum(grad, axis=0, keepdims=True)
    grad = norm_back(grad * gain1, normed1, inverse1)
    dz1_ref[...] = grad
    dbranch = grad.astype(low)
    dbranch_ref[...] = dbranch
    da_ref[...] = dot_nt(dbranch, out_w[...]).astype(low)


def middle(plan, ids, attended, tokens, cot, vectors, sources, hidden):
    rows, width = tokens.shape
    block = TOKEN_BLOCK
    tile = lambda w: pl.BlockSpec((block, w), lambda i, *_: (i, 0))
    whole = pl.BlockSpec((8, width), lambda i, *_: (0, 0))
    return pl.pallas_call(
        functools.partial(middle_kernel, plan, len(sources)),
        grid_spec=pltpu.PrefetchScalarGridSpec(
            num_scalar_prefetch=1,
            grid=(rows // block,),
            in_specs=[tile(width), tile(width), tile(width), whole]
            + [pl.BlockSpec(memory_space=pl.ANY)] * len(sources),
            out_specs=[
                tile(width),
                tile(width),
                tile(width),
                tile(width),
                tile(hidden),
                tile(width),
                tile(hidden),
                tile(hidden),
                tile(width),
                whole,
            ],
            scratch_shapes=[
                pltpu.VMEM((width, width), low),
                pltpu.VMEM((hidden // width, width, width), low),
                pltpu.VMEM((hidden // width, width, width), low),
                pltpu.VMEM((hidden, width), low),
                pltpu.VMEM((block, hidden), full),
                pltpu.VMEM((block, hidden), full),
                pltpu.SemaphoreType.DMA((4,)),
            ],
        ),
        out_shape=[
            shape((rows, width), low),
            shape((rows, width), full),
            shape((rows, width), low),
            shape((rows, width), low),
            shape((rows, hidden), low),
            shape((rows, width), low),
            shape((rows, hidden), low),
            shape((rows, hidden), low),
            shape((rows, width), low),
            shape((8, width), full),
        ],
        compiler_params=params(),
        cost_estimate=pl.CostEstimate(
            flops=2 * rows * width * (2 * width + 6 * hidden),
            bytes_accessed=40 << 20,
            transcendentals=rows * hidden,
        ),
        name="middle",
    )(ids, attended, tokens, cot, vectors, *sources)


def weight_grad_kernel(a_ref, b_ref, o_ref):
    o_ref[...] = dot_tn(a_ref[...], b_ref[...]).astype(o_ref.dtype)


def weight_grad(a, b, tile_a=768, tile_b=768):
    rows, size_a = a.shape
    size_b = b.shape[1]
    return pl.pallas_call(
        weight_grad_kernel,
        grid=(size_a // tile_a, size_b // tile_b),
        in_specs=[
            pl.BlockSpec((rows, tile_a), lambda i, j: (0, i)),
            pl.BlockSpec((rows, tile_b), lambda i, j: (0, j)),
        ],
        out_specs=pl.BlockSpec((tile_a, tile_b), lambda i, j: (i, j)),
        out_shape=shape((size_a, size_b), low),
        compiler_params=params(),
        cost_estimate=pl.CostEstimate(
            flops=2 * rows * size_a * size_b,
            bytes_accessed=2 * (rows * (size_a + size_b) + size_a * size_b),
            transcendentals=0,
        ),
        name="weight_grad",
    )(a, b)


def joint_kernel(reach, dq_ref, own_ref, prior_ref, next_ref, cos_ref, sin_ref, dj_ref):
    block, width = dq_ref.shape
    step = pl.program_id(0)
    early = step < pl.num_programs(0) // 2
    cosine = cos_ref[...]
    sine = sin_ref[...]
    for at in range(0, width, PAIR):
        lanes = slice(at, at + PAIR)
        near = [
            jnp.where(early, prior_ref[i, :, lanes], next_ref[i, :, lanes]).astype(full)
            for i in range(2)
        ]
        dj_ref[:, lanes] = turn_back(dq_ref[:, lanes], cosine, sine).astype(low)
        dj_ref[:, width + at : width + at + PAIR] = turn_back(
            own_ref[0, :, lanes] + near[0], cosine, sine
        ).astype(low)
        dj_ref[:, 2 * width + at : 2 * width + at + PAIR] = (
            own_ref[1, :, lanes] + near[1]
        ).astype(low)


def joint(dq, own, prior, following, cosine, sine):
    rows, width = dq.shape
    reach = prior.shape[1]
    block = TOKEN_BLOCK
    half = reach // block
    tile = lambda w: pl.BlockSpec((block, w), lambda i: (i, 0))
    inner = pl.BlockSpec((block, PAIR), lambda i: (i + half, 0))
    return pl.pallas_call(
        functools.partial(joint_kernel, reach),
        grid=(rows // block,),
        in_specs=[
            tile(width),
            pl.BlockSpec((2, block, width), lambda i: (0, i, 0)),
            pl.BlockSpec((2, block, width), lambda i: (0, jnp.minimum(i, half - 1), 0)),
            pl.BlockSpec((2, block, width), lambda i: (0, jnp.maximum(i - half, 0), 0)),
            inner,
            inner,
        ],
        out_specs=tile(3 * width),
        out_shape=shape((rows, 3 * width), low),
        compiler_params=params(),
        cost_estimate=pl.CostEstimate(
            flops=12 * rows * width, bytes_accessed=24 * rows * width, transcendentals=0
        ),
        name="joint",
    )(dq, own, prior, following, cosine, sine)


def input_grad_kernel(plan, sources, ids, dj_ref, dz1_ref, *refs):
    srcs = refs[:sources]
    out_ref, weight, sems = refs[sources:]
    copies = plan(ids, srcs, weight, sems)

    @pl.when(pl.program_id(0) == 0)
    def _():
        for copy in copies:
            copy.start()
        for copy in copies:
            copy.wait()

    width = dz1_ref.shape[1]
    out = dz1_ref[...]
    for i in range(3):
        out = out + dot_nt(dj_ref[:, i * width : (i + 1) * width], weight[i])
    out_ref[...] = out


def input_grad(plan, ids, dj, dz1, sources):
    rows, width = dz1.shape
    block = TOKEN_BLOCK
    tile = lambda w: pl.BlockSpec((block, w), lambda i, *_: (i, 0))
    return pl.pallas_call(
        functools.partial(input_grad_kernel, plan, len(sources)),
        grid_spec=pltpu.PrefetchScalarGridSpec(
            num_scalar_prefetch=1,
            grid=(rows // block,),
            in_specs=[tile(3 * width), tile(width)]
            + [pl.BlockSpec(memory_space=pl.ANY)] * len(sources),
            out_specs=tile(width),
            scratch_shapes=[
                pltpu.VMEM((3, width, width), low),
                pltpu.SemaphoreType.DMA((1,)),
            ],
        ),
        out_shape=shape((rows, width), full),
        compiler_params=params(),
        cost_estimate=pl.CostEstimate(
            flops=6 * rows * width * width, bytes_accessed=14 * rows * width, transcendentals=0
        ),
        name="input_grad",
    )(ids, dj, dz1, *sources)


def whole_joint_plan(ids, srcs, weight, sems):
    width = weight.shape[1]
    return [
        pltpu.make_async_copy(srcs[0].at[:, i * width : (i + 1) * width], weight.at[i], sems.at[0])
        for i in range(3)
    ]


def whole_middle_plan(ids, srcs, weights, sems):
    out_w, gate_w, up_w, down_w = weights
    parts, _, width = gate_w.shape
    columns = lambda src, dst, sem: [
        pltpu.make_async_copy(src.at[:, i * width : (i + 1) * width], dst.at[i], sem)
        for i in range(parts)
    ]
    return [
        [pltpu.make_async_copy(srcs[0], out_w, sems.at[0])],
        columns(srcs[1], gate_w, sems.at[1]),
        columns(srcs[2], up_w, sems.at[2]),
        [pltpu.make_async_copy(srcs[3], down_w, sems.at[3])],
    ]


def shards(
    tokens,
    lengths,
    qkv_weight,
    out_weight,
    gate_weight,
    up_weight,
    down_weight,
    norm1_gain,
    norm1_bias,
    norm2_gain,
    norm2_bias,
    cotangent,
):
    rows, width = tokens.shape
    hidden = gate_weight.shape[1]
    size = lax.axis_size("fsdp")
    me = lax.axis_index("fsdp")
    up = [(i, i + 1) for i in range(size - 1)]
    down = [(i + 1, i) for i in range(size - 1)]
    tokens_ext = jnp.concatenate(
        [
            lax.ppermute(tokens[rows - REACH :], "fsdp", up),
            tokens,
            lax.ppermute(tokens[:REACH], "fsdp", down),
        ],
        axis=0,
    )

    doc_lengths = lengths[0]
    ends = jnp.cumsum(doc_lengths)
    index = me * rows - REACH + jnp.arange(rows + 2 * REACH, dtype=jnp.int32)
    after = (index[:, None] >= ends[None, :]).astype(jnp.int32)
    starts = jnp.sum(after * doc_lengths[None, :], axis=1)
    cosine, sine = tables(index - starts)
    own_starts = starts[REACH : REACH + rows]
    own_index = index[REACH : REACH + rows]
    stops = jnp.min(
        jnp.where(ends[None, :] > own_index[:, None], ends[None, :], size * rows), axis=1
    )
    base = me * rows - REACH
    bounds = jnp.stack(
        [
            jnp.maximum(own_starts, own_index - REACH) - base,
            jnp.minimum(stops, own_index + REACH + 1) - base,
        ]
    ).astype(jnp.int32)

    ids = jnp.zeros((8,), jnp.int32)
    gather = lambda w: lax.all_gather(w.astype(low), "fsdp", axis=0, tiled=True)
    qkv_full = gather(qkv_weight)
    weights = [gather(w) for w in (out_weight, gate_weight, up_weight, down_weight)]
    vectors = jnp.stack([norm1_gain, norm1_bias, norm2_gain, norm2_bias])
    vectors = lax.all_gather(vectors.astype(low), "fsdp", axis=1, tiled=True).astype(full)
    vectors = jnp.concatenate([vectors, vectors], axis=0)

    queries, keys, values = project(
        whole_joint_plan, ids, tokens_ext, cosine, sine, [qkv_full], rows
    )
    attended, lse = attend(bounds, queries, keys, values)
    result, dz1, dattended, hidden_low, product, dfeed, dgate, dlift, dbranch, gains = middle(
        whole_middle_plan, ids, attended, tokens, cotangent, vectors, weights, hidden
    )
    spread = lambda g: lax.psum_scatter(g, "fsdp", scatter_dimension=0, tiled=True)
    share_down = spread(weight_grad(product, dfeed))
    share_gate = spread(weight_grad(hidden_low, dgate))
    share_up = spread(weight_grad(hidden_low, dlift))
    share_out = spread(weight_grad(attended, dbranch))
    share_gains = lax.psum_scatter(gains[:4], "fsdp", scatter_dimension=1, tiled=True)

    dq, dkv, to_prior, to_next = attend_back(
        bounds, queries, keys, values, attended, dattended, lse
    )
    from_prior = lax.ppermute(to_next, "fsdp", up)
    from_next = lax.ppermute(to_prior, "fsdp", down)
    djoint = joint(dq, dkv, from_prior, from_next, cosine, sine)
    share_qkv = spread(weight_grad(tokens, djoint))
    grad_tokens = input_grad(whole_joint_plan, ids, djoint, dz1, [qkv_full])
    summed = lax.psum(
        tuple(
            s.astype(full)
            for s in (share_qkv, share_out, share_gate, share_up, share_down, share_gains)
        ),
        "rep",
    )
    return (result, grad_tokens, *summed[:5], *(summed[5][i] for i in range(4)))


def solution(mesh):
    rows = P(("rep", "fsdp"), None)
    matrix = P("fsdp", None)
    vector = P("fsdp")
    return jax.shard_map(
        shards,
        mesh=mesh,
        in_specs=(rows, P("rep", None)) + (matrix,) * 5 + (vector,) * 4 + (rows,),
        out_specs=(rows, rows) + (matrix,) * 5 + (vector,) * 4,
        check_vma=False,
    )
```

time: 1340 us -> 780 us (0.58)
  matrix products: 388 us -> 0 us
  Pallas kernels: 0 us -> 211 us
  waiting for transfers between devices: 493 us -> 311 us
  local copies, waits for them, and re-layouts: 160 us -> 6.14 us
  other arithmetic: 159 us -> 16.8 us
  blocking collectives: 95.7 us -> 202 us
    dot_general x29 -> x0, matrix products: 388 us -> none  [the longest x4 66.3 us: block_scores(): jnp.einsum('qhd,khd->hqk', query_rows, key_rows, preferred_element_type=j...]
    pallas_call x0 -> x11, Pallas kernels: none -> 211 us  [the longest x1 53.6 us: middle(): pl.pallas_call(functools.partial(middle_kernel, plan, len(sources)), grid...]
    psum x1, blocking collectives: 10.6 us -> 159 us  [shards(): lax.psum(tuple((s.astype(full) for s in (share_qkv, share_out, share_gate...]
    reduce_scatter x4 -> x5, waiting for transfers between devices: 336 us -> 188 us  [shards(): lax.psum_scatter(g, 'fsdp', scatter_dimension=0, tiled=True)]
    unnamed x2 -> x0, blocking collectives: 85.1 us -> none
    all_gather x5, waiting for transfers between devices: 37.4 us -> 119 us  [shards(): gather = lambda w: lax.all_gather(w.astype(low), 'fsdp', axis=0, tiled=True)]
    psum x1 -> x0, waiting for transfers between devices: 72.8 us -> none  [shards(): lax.psum((share_qkv, share_out, share_gate, share_up, share_down, share_g...]
    convert_element_type x17 -> x6, other arithmetic: 75 us -> 7.76 us  [the longest x5 7.76 us: shards(): gather = lambda w: lax.all_gather(w.astype(low), 'fsdp', axis=0, tiled=True)]
  transfers between devices with their start and end apart: 15 -> 15, of which waited for: 7 -> 9; matrix products, arithmetic and copies ran while one was open for 20% -> 2% of each run, Pallas kernels for 0% -> 20%
where the time goes in v1:
time: 780 us; the launch traced here: 770 us
  waiting for transfers between devices  311 us (40%)
  Pallas kernels  211 us (27%)
  blocking collectives  202 us (26%)
  other arithmetic  16.8 us (2%)
  between operations  14.6 us (2%)
    reduce_scatter x5, waiting for transfers between devices, shards(): lax.psum_scatter(g, 'fsdp', scatter_dimension=0, tiled=True)  188 us
    psum x1, blocking collectives, shards(): lax.psum(tuple((s.astype(full) for s in (share_qkv, share_out, share_gate...  159 us
    all_gather x5, waiting for transfers between devices, shards(): gather = lambda w: lax.all_gather(w.astype(low), 'fsdp', axis=0, tiled=True)  119 us
    pallas_call x1, Pallas kernels, middle(): pl.pallas_call(functools.partial(middle_kernel, plan, len(sources)), grid...  53.6 us
    pallas_call x1, Pallas kernels, attend_back(): pl.pallas_call(functools.partial(attend_back_kernel, chunk), grid=(pairs,...  46.5 us
    all_gather x1, blocking collectives, shards(): lax.all_gather(vectors.astype(low), 'fsdp', axis=1, tiled=True).astype(full)  43 us
    pallas_call x5, Pallas kernels, weight_grad(): pl.pallas_call(weight_grad_kernel, grid=(size_a // tile_a, size_b // tile...  40 us
    pallas_call x1, Pallas kernels, attend(): pl.pallas_call(functools.partial(attend_kernel, chunk), grid=(pairs,), in...  36 us
  transfers between devices with their start and end apart: 15, of which 9 were waited for; matrix products, arithmetic and copies ran while one was open for 2% of the time, Pallas kernels for 20%

profile of v1, /device:TPU:0, one launch (start us, length us, event | category | flops | bytes accessed | tf_op | source)
XLA Modules:
  0.0 769.8 jit_solution(18437662533515937955)
XLA Ops:
  7.2 2.1 convert_element_type.49
  9.3 0.0 all-gather.9.cloned.1.call-start
  9.4 1.6 convert_element_type.50
  11.1 0.9 convert_element_type.51
  12.1 2.3 convert_element_type.52
  14.4 0.0 all-gather.15.cloned.1.call-start
  14.5 0.9 convert_element_type.53
  15.4 1.2 fusion.6
  16.7 2.4 collective-permute-start
  19.1 1.3 collective-permute-start.1
  20.5 43.0 %all-gather = bf16[8,96,4]{1,2,0:T(4,128)(2,1)S(1)} all-gather(bf16[1,96,4]{1,2,0:T(4,128)(2,1)S(1)} %maximum_bitcast_fusion), channel_id=1, replica_groups=mesh['rep'=4,'fsdp'=8] {'fsdp'}, dimensions={0}, use_global_device_ids=true | all-gather | bytes 6912 | tf_op jit(solution)/shard_map/all_gather | solution.py:680
  63.5 0.1 reshape.87
  63.6 0.2 reduce-window.8
  63.7 0.1 select_reduce_fusion
  63.9 0.1 select_reduce_fusion.1
  64.0 0.6 pad_add_fusion.bounds_ref
  64.6 0.6 maximum_convert_fusion.vec_ref
  65.2 5.6 fusion
  70.8 1.8 pad_maximum_fusion.tok_ref
  72.6 0.5 broadcast_4_ids.2.ids
  73.1 15.5 %project.1 = (bf16[1024,768]{1,0:T(8,128)(2,1)}, bf16[2048,768]{1,0:T(8,128)(2,1)}, bf16[2048,768]{1,0:T(8,128)(2,1)}) custom-call(s32[8]{0:T(128)} %broadcast_4_ids.2.ids, bf16[2048,768]{1,0:T(8,128)(2,1)} %pad_maximum_fusion.tok_ref, f32[2048,128]{1,0:T(8,128)} %get-tuple-element.58.cos_ref, f32[2048,128]{1,0:T(8,128)} %get-tuple-element.57.sin_ref, ...), custom_call_target="tpu_custom_call" | custom-call | flops 6039797760 | bytes 18874368 | tf_op jit(solution)/shard_map/project/pallas_call | solution.py:106
  88.7 36.0 %attend.1 = (bf16[1024,768]{1,0:T(8,128)(2,1)}, f32[6,2,1024]{2,1,0:T(2,128)}) custom-call(s32[2,1024]{1,0:T(2,128)} %pad_add_fusion.bounds_ref, bf16[1024,768]{1,0:T(8,128)(2,1)} %get-tuple-element.30.q_ref, bf16[2048,768]{1,0:T(8,128)(2,1)} %get-tuple-element.31.k_ref, bf16[2048,768]{1,0:T(8,128)(2,1)} %get-tuple-element.32.v_ref), custom_call_target="tpu_custom_call" | custom-call | flops 16106127360 | bytes 6291456 | tf_op jit(solution)/shard_map/attend/pallas_call | solution.py:193
  124.7 15.3 %all-gather.11.cloned.1.call-done.refs_1_ = bf16[768,3072]{1,0:T(8,128)(2,1)} async-done(((bf16[96,3072]{1,0:T(8,128)(2,1)}), bf16[768,3072]{1,0:T(8,128)(2,1)}) %all-gather.11.cloned.1.call-update) | async-done | bytes 4718608 | tf_op jit(solution)/shard_map/all_gather | solution.py:676
  139.9 52.0 %all-gather.13.cloned.1.call-done.refs_2_ = bf16[768,3072]{1,0:T(8,128)(2,1)} async-done(((bf16[96,3072]{1,0:T(8,128)(2,1)}), bf16[768,3072]{1,0:T(8,128)(2,1)}) %all-gather.13.cloned.1.call-update) | async-done | bytes 4718608 | tf_op jit(solution)/shard_map/all_gather | solution.py:676
  192.0 52.0 %all-gather.15.cloned.1.call-done.refs_3_ = bf16[3072,768]{1,0:T(8,128)(2,1)} async-done(((bf16[384,768]{1,0:T(8,128)(2,1)}), bf16[3072,768]{1,0:T(8,128)(2,1)}) %all-gather.15.cloned.1.call-update) | async-done | bytes 4718608 | tf_op jit(solution)/shard_map/all_gather | solution.py:676
  244.0 53.6 %middle.1 = (bf16[1024,768]{1,0:T(8,128)(2,1)}, f32[1024,768]{1,0:T(8,128)}, bf16[1024,768]{1,0:T(8,128)(2,1)}, bf16[1024,768]{1,0:T(8,128)(2,1)}, bf16[1024,307...) custom-call(s32[8]{0:T(128)} %broadcast_4_ids.2.ids, ...), custom_call_target="tpu_custom_call" | custom-call | flops 31406948352 | bytes 41943040 | tf_op jit(solution)/shard_map/middle/pallas_call | solution.py:433
  297.6 0.7 slice.31
  298.3 0.9 copy.26
  299.3 4.3 weight_grad.6
  303.7 46.5 %attend_back.1 = (f32[1024,768]{1,0:T(8,128)}, f32[2,1024,768]{2,1,0:T(8,128)}, bf16[2,512,768]{2,1,0:T(8,128)(2,1)}, bf16[2,512,768]{2,1,0:T(8,128)(2,1)}) custom-call(s32[2,1024]{1,0:T(2,128)} %pad_add_fusion.bounds_ref, bf16[1024,768]{1,0:T(8,128)(2,1)} %get-tuple-element.30.q_ref, bf16[2048,768]{1,0:T(8,128)(2,1)} %get-tuple-element.31.k_ref, ...), custom_call_target="tpu_custom_call" | custom-call | flops 40265318400 | bytes 15728640 | tf_op jit(solution)/shard_map/attend_back/pallas_call | solution.py:295
  350.2 2.2 collective-permute-start.2
  352.5 1.3 collective-permute-start.3
  353.8 1.8 collective-permute-done.2.prior_ref
  355.6 2.4 collective-permute-done.3.next_ref
  358.0 1.2 copy-done.2
  359.2 8.8 %joint.1.dj_ref.b_ref = bf16[1024,2304]{1,0:T(8,128)(2,1)} custom-call(f32[1024,768]{1,0:T(8,128)} %get-tuple-element.37.dq_ref, f32[2,1024,768]{2,1,0:T(8,128)} %get-tuple-element.38.own_ref, bf16[2,512,768]{2,1,0:T(8,128)(2,1)} %copy-done.1, bf16[2,512,768]{2,1,0:T(8,128)(2,1)} %copy-done.2, f32[2048,128]{1,0:T(8,128)} %get-tuple-element.58.cos_ref, ...), custom_call_target="tpu_custom_call" | custom-call | flops 9437184 | bytes 18874368 | tf_op jit(solution)/shard_map/joint/pallas_call | solution.py:538
  368.0 7.7 %weight_grad.5 = bf16[768,2304]{1,0:T(8,128)(2,1)} custom-call(bf16[1024,768]{1,0:T(8,128)(2,1)} %a_ref.1, bf16[1024,2304]{1,0:T(8,128)(2,1)} %joint.1.dj_ref.b_ref), custom_call_target="tpu_custom_call" | custom-call | flops 3623878656 | bytes 9830400 | tf_op jit(solution)/shard_map/weight_grad/pallas_call | solution.py:491
  375.7 9.3 %weight_grad.8 = bf16[768,3072]{1,0:T(8,128)(2,1)} custom-call(bf16[1024,768]{1,0:T(8,128)(2,1)} %get-tuple-element.43.a_ref, bf16[1024,3072]{1,0:T(8,128)(2,1)} %get-tuple-element.45.b_ref), custom_call_target="tpu_custom_call" | custom-call | flops 4831838208 | bytes 12582912 | tf_op jit(solution)/shard_map/weight_grad/pallas_call | solution.py:491
  385.1 9.5 %weight_grad.7 = bf16[768,3072]{1,0:T(8,128)(2,1)} custom-call(bf16[1024,768]{1,0:T(8,128)(2,1)} %get-tuple-element.43.a_ref, bf16[1024,3072]{1,0:T(8,128)(2,1)} %get-tuple-element.44.b_ref), custom_call_target="tpu_custom_call" | custom-call | flops 4831838208 | bytes 12582912 | tf_op jit(solution)/shard_map/weight_grad/pallas_call | solution.py:491
  394.7 9.2 %weight_grad.9 = bf16[3072,768]{1,0:T(8,128)(2,1)} custom-call(bf16[1024,3072]{1,0:T(8,128)(2,1)} %get-tuple-element.46.a_ref, bf16[1024,768]{1,0:T(8,128)(2,1)} %get-tuple-element.47.b_ref), custom_call_target="tpu_custom_call" | custom-call | flops 4831838208 | bytes 12582912 | tf_op jit(solution)/shard_map/weight_grad/pallas_call | solution.py:491
  403.9 0.9 copy.27
  404.8 10.6 %input_grad.1 = f32[1024,768]{1,0:T(8,128)} custom-call(s32[8]{0:T(128)} %broadcast_4_ids.2.ids, bf16[1024,2304]{1,0:T(8,128)(2,1)} %joint.1.dj_ref.b_ref, f32[1024,768]{1,0:T(8,128)} %get-tuple-element.41.dz1_ref, bf16[768,2304]{1,0:T(8,128)(2,1)} %all-gather.7.cloned.1.call-done.refs_0_), custom_call_target="tpu_custom_call" | custom-call | flops 3623878656 | bytes 11010048 | tf_op jit(solution)/shard_map/input_grad/pallas_call | solution.py:582
  415.4 20.5 %reduce-scatter.9.cloned.1.call-done = bf16[96,2304]{1,0:T(8,128)(2,1)} async-done(((bf16[768,2304]{1,0:T(8,128)(2,1)}), bf16[96,2304]{1,0:T(8,128)(2,1)}) %reduce-scatter.9.cloned.1.call-update) | async-done | bytes 442384 | tf_op jit(solution)/shard_map/reduce_scatter | solution.py:690
  435.9 55.8 %reduce-scatter.15.cloned.1.call-done = bf16[96,3072]{1,0:T(8,128)(2,1)} async-done(((bf16[768,3072]{1,0:T(8,128)(2,1)}), bf16[96,3072]{1,0:T(8,128)(2,1)}) %reduce-scatter.15.cloned.1.call-update) | async-done | bytes 589840 | tf_op jit(solution)/shard_map/reduce_scatter | solution.py:690
  491.7 55.5 %reduce-scatter.13.cloned.1.call-done = bf16[96,3072]{1,0:T(8,128)(2,1)} async-done(((bf16[768,3072]{1,0:T(8,128)(2,1)}), bf16[96,3072]{1,0:T(8,128)(2,1)}) %reduce-scatter.13.cloned.1.call-update) | async-done | bytes 589840 | tf_op jit(solution)/shard_map/reduce_scatter | solution.py:690
  547.3 55.7 %reduce-scatter.17.cloned.1.call-done = bf16[384,768]{1,0:T(8,128)(2,1)} async-done(((bf16[3072,768]{1,0:T(8,128)(2,1)}), bf16[384,768]{1,0:T(8,128)(2,1)}) %reduce-scatter.17.cloned.1.call-update) | async-done | bytes 589840 | tf_op jit(solution)/shard_map/reduce_scatter | solution.py:690
  602.9 159.4 %all-reduce.2 = (f32[96,2304]{1,0:T(8,128)}, f32[96,768]{1,0:T(8,128)}, f32[96,3072]{1,0:T(8,128)}, f32[96,3072]{1,0:T(8,128)}, f32[384,768]{1,0:T(8,128)}, /*index=5*/f32[4,96]{1,0:T(4,128)S(1)}) all-reduce(bf16[96,2304]{1,0:T(8,128)(2,1)} %reduce-scatter.9.cloned.1.call-done, ...), channel_id=1, replica_groups=mesh['rep'=4,'fsdp'=8] {'rep'}, use_global_device_ids=true, to_apply=%region_4.5 | all-reduce | flops 1180032 | bytes 7080960 | tf_op jit(solution)/shard_map/psum | solution.py:705
  762.3 0.5 slice_bitcast_fusion
  (54 shorter events, 0.7 us)
Async XLA Ops:
  7.2 3.9 copy-start.3
  7.2 65.4 %all-gather.7.cloned.1.call-start = ((), (), s32[]{:S(2)}) async-start(), calls=%async_computation.6 | async-start | bytes 3981312 | tf_op jit(solution)/shard_map/all_gather | solution.py:676
  9.3 115.3 %all-gather.9.cloned.1.call-start = ((), (), s32[]{:S(2)}) async-start(), calls=%async_computation.7 | async-start | bytes 1327104 | tf_op jit(solution)/shard_map/all_gather | solution.py:676
  11.1 4.4 copy-start
  11.1 128.8 %all-gather.11.cloned.1.call-start = ((), (), s32[]{:S(2)}) async-start(), calls=%async_computation.8 | async-start | bytes 5308416 | tf_op jit(solution)/shard_map/all_gather | solution.py:676
  12.0 2.4 copy-start.4
  12.0 179.9 %all-gather.13.cloned.1.call-start = ((), (), s32[]{:S(2)}) async-start(), calls=%async_computation.9 | async-start | bytes 5308416 | tf_op jit(solution)/shard_map/all_gather | solution.py:676
  14.4 6.0 copy-start.6
  14.4 6.0 copy-start.7
  14.4 6.1 copy-start.8
  14.4 6.1 copy-start.9
  14.4 49.2 %copy-start.5 = (s32[1,8]{1,0:T(1,128)S(1)}, s32[1,8]{1,0:T(1,128)}, u32[]{:S(2)}) copy-start(s32[1,8]{1,0:T(1,128)} %param.13) | copy-start | bytes 100
  14.4 229.6 %all-gather.15.cloned.1.call-start = ((), (), s32[]{:S(2)}) async-start(), calls=%async_computation.10 | async-start | bytes 5308416 | tf_op jit(solution)/shard_map/all_gather | solution.py:676
  15.4 388.6 %reduce-scatter.19.cloned.1.call-start = ((), (), s32[]{:S(2)}) async-start(), calls=%async_computation.16 | async-start | bytes 442368
  16.7 54.1 %collective-permute-start = (bf16[512,768]{1,0:T(8,128)(2,1)}, bf16[512,768]{1,0:T(8,128)(2,1)S(1)}, u32[]{:S(2)}, u32[]{:S(2)}) collective-permute-start(bf16[512,768]{1,0:T(8,128)(2,1)} %get-tuple-element.55), channel_id=1, source_target_pairs={{0,1},{1,2},{2,3},{3,4},{4,5},{5,6},{6,7},{8,9},{9,10},{10,11},{11... | collective-permute-start | bytes 2359304 | tf_op jit(solution)/shard_map/ppermute | solution.py:649
  19.1 51.7 %collective-permute-start.1 = (bf16[512,768]{1,0:T(8,128)(2,1)}, bf16[512,768]{1,0:T(8,128)(2,1)S(1)}, u32[]{:S(2)}, u32[]{:S(2)}) collective-permute-start(bf16[512,768]{1,0:T(8,128)(2,1)} %get-tuple-element.56), channel_id=1, source_target_pairs={{1,0},{2,1},{3,2},{4,3},{5,4},{6,5},{7,6},{9,8},{10,9},{11,10},{12... | collective-permute-start | bytes 2359304 | tf_op jit(solution)/shard_map/ppermute | solution.py:651
  299.3 116.2 %reduce-scatter.11.cloned.1.call-start = ((), (), s32[]{:S(2)}) async-start(), calls=%async_computation.12 | async-start | bytes 1327104 | tf_op jit(solution)/shard_map/reduce_scatter | solution.py:690
  303.7 132.3 %reduce-scatter.9.cloned.1.call-start = ((), (), s32[]{:S(2)}) async-start(), calls=%async_computation.11 | async-start | bytes 3981312 | tf_op jit(solution)/shard_map/reduce_scatter | solution.py:690
  350.2 5.4 collective-permute-start.2
  352.5 5.5 collective-permute-start.3
  355.6 2.4 copy-start.1
  358.0 1.2 copy-start.2
  375.7 116.0 %reduce-scatter.15.cloned.1.call-start = ((), (), s32[]{:S(2)}) async-start(), calls=%async_computation.14 | async-start | bytes 5308416 | tf_op jit(solution)/shard_map/reduce_scatter | solution.py:690
  385.0 162.3 %reduce-scatter.13.cloned.1.call-start = ((), (), s32[]{:S(2)}) async-start(), calls=%async_computation.13 | async-start | bytes 5308416 | tf_op jit(solution)/shard_map/reduce_scatter | solution.py:690
  394.6 208.3 %reduce-scatter.17.cloned.1.call-start = ((), (), s32[]{:S(2)}) async-start(), calls=%async_computation.15 | async-start | bytes 5308416 | tf_op jit(solution)/shard_map/reduce_scatter | solution.py:690
Sparse Core Ops, SparseCore 0:
  9.7 49.1 all-gather.6
  61.1 25.0 all-gather.8
  88.4 51.4 all-gather.10
  141.4 50.5 all-gather.12
  193.4 50.5 all-gather.14
  299.4 29.4 reduce-scatter.18
  331.8 31.4 reduce-scatter.10
  375.8 60.0 reduce-scatter.8
  438.2 53.4 reduce-scatter.14
  493.9 53.3 reduce-scatter.12
  549.6 53.3 reduce-scatter.16

commit v2 on v1

--- a/solution.py
+++ b/solution.py
@@ -15,6 +15,7 @@
 PAIR = 2 * HEAD
 QUERY_BLOCK = 256
 TOKEN_BLOCK = 256
+FORCE_WHOLE = False
 VMEM = 56 * 1024 * 1024
 
 epsilon = 1e-06
@@ -42,6 +43,10 @@
 
 def shape(dims, dtype):
     return jax.ShapeDtypeStruct(dims, dtype)
+
+
+def cost(micros):
+    return pl.CostEstimate(flops=int(micros * 1.15e9), bytes_accessed=1 << 20, transcendentals=0)
 
 
 def tables(position):
@@ -71,14 +76,12 @@
     srcs = refs[:sources]
     q_ref, k_ref, v_ref, weight, sems = refs[sources:]
     step = pl.program_id(0)
-    copies = plan(ids, srcs, weight, sems)
 
     @pl.when(step == 0)
     def _():
-        for copy in copies:
+        for copy in plan(ids, srcs, weight, sems.at[0]):
             copy.start()
-        for copy in copies:
-            copy.wait()
+        pltpu.make_async_copy(weight, weight, sems.at[0]).wait()
 
     width = tok_ref.shape[1]
     rows = tok_ref[...]
@@ -110,19 +113,22 @@
             grid=(ext // block,),
             in_specs=[tile(width), tile(PAIR), tile(PAIR)]
             + [pl.BlockSpec(memory_space=pl.ANY)] * len(sources),
-            out_specs=[inner, tile(width), tile(width)],
-            scratch_shapes=[
-                pltpu.VMEM((3, width, width), low),
-                pltpu.SemaphoreType.DMA((1,)),
+            out_specs=[
+                inner,
+                tile(width),
+                tile(width),
+                pl.BlockSpec((4, width, width), lambda i, *_: (0, 0, 0)),
             ],
+            scratch_shapes=[pltpu.SemaphoreType.DMA((1,))],
         ),
-        out_shape=[shape((rows, width), low), shape((ext, width), low), shape((ext, width), low)],
+        out_shape=[
+            shape((rows, width), low),
+            shape((ext, width), low),
+            shape((ext, width), low),
+            shape((4, width, width), low),
+        ],
         compiler_params=params(),
-        cost_estimate=pl.CostEstimate(
-            flops=2 * width * width * (2 * ext + rows),
-            bytes_accessed=12 * ext * width,
-            transcendentals=0,
-        ),
+        cost_estimate=cost(15),
         name="project",
     )(ids, tokens, cosine, sine, *sources)
 
@@ -140,7 +146,8 @@
     return jnp.where((lane >= HEAD) if head else (lane < HEAD), x, jnp.zeros_like(x))
 
 
-def attend_kernel(chunk, bounds_ref, q_ref, k_ref, v_ref, o_ref, lse_ref, bias_ref, vt_ref, s_ref):
+def attend_kernel(chunk, bounds_ref, q_ref, k_ref, v_ref, *refs):
+    o_ref, lse_ref, bias_ref, vt_ref, s_ref = refs[-5:]
     rows = q_ref.shape[0]
     block = QUERY_BLOCK
     blocks = rows // block
@@ -182,33 +189,31 @@
         o_ref[b * block : (b + 1) * block, :] = jnp.concatenate(out, axis=0).T.astype(low)
 
 
-def attend(bounds, q, k, v, chunk=640):
+def attend(bounds, q, k, v, first, pairs, before=None, chunk=640):
     rows, width = q.shape
     ext = k.shape[0]
-    pairs = width // PAIR
     blocks = rows // QUERY_BLOCK
     span = ext - rows + QUERY_BLOCK
-    own = pl.BlockSpec((rows, PAIR), lambda p: (0, p))
-    wide = pl.BlockSpec((ext, PAIR), lambda p: (0, p))
+    own = pl.BlockSpec((rows, PAIR), lambda p: (0, p + first))
+    wide = pl.BlockSpec((ext, PAIR), lambda p: (0, p + first))
+    before = () if before is None else tuple(before)
     return pl.pallas_call(
         functools.partial(attend_kernel, chunk),
         grid=(pairs,),
-        in_specs=[pl.BlockSpec((2, rows), lambda p: (0, 0)), own, wide, wide],
-        out_specs=[own, pl.BlockSpec((1, 2, rows), lambda p: (p, 0, 0))],
-        out_shape=[shape((rows, width), low), shape((pairs, 2, rows), full)],
+        in_specs=[pl.BlockSpec((2, rows), lambda p: (0, 0)), own, wide, wide]
+        + [pl.BlockSpec(memory_space=pl.ANY)] * len(before),
+        out_specs=[own, pl.BlockSpec((1, 2, rows), lambda p: (p + first, 0, 0))],
+        out_shape=[shape((rows, width), low), shape((width // PAIR, 2, rows), full)],
+        input_output_aliases={4 + i: i for i in range(len(before))},
         scratch_shapes=[
             pltpu.VMEM((blocks, span, QUERY_BLOCK), full),
             pltpu.VMEM((PAIR, ext), low),
             pltpu.VMEM((2, span, QUERY_BLOCK), full),
         ],
         compiler_params=params(),
-        cost_estimate=pl.CostEstimate(
-            flops=16 * rows * span * width,
-            bytes_accessed=4 * ext * width,
-            transcendentals=rows * span * width // HEAD,
-        ),
+        cost_estimate=cost(6 * pairs),
         name="attend",
-    )(bounds, q, k, v)
+    )(bounds, q, k, v, *before)
 
 
 def attend_back_kernel(
@@ -220,15 +225,9 @@
     o_ref,
     do_ref,
     lse_ref,
-    dq_ref,
-    own_ref,
-    prior_ref,
-    next_ref,
-    bias_ref,
-    kt_ref,
-    dk_ref,
-    dv_ref,
+    *refs,
 ):
+    dq_ref, own_ref, prior_ref, next_ref, bias_ref, kt_ref, dk_ref, dv_ref = refs[-8:]
     rows = q_ref.shape[0]
     ext = k_ref.shape[0]
     block = QUERY_BLOCK
@@ -282,16 +281,17 @@
         next_ref[i] = ref[reach + rows :, :].astype(low)
 
 
-def attend_back(bounds, q, k, v, o, do, lse, chunk=1280):
+def attend_back(bounds, q, k, v, o, do, lse, first, pairs, halo, before=None, chunk=1280):
     rows, width = q.shape
     ext = k.shape[0]
-    pairs = width // PAIR
     blocks = rows // QUERY_BLOCK
     reach = (ext - rows) // 2
     span = ext - rows + QUERY_BLOCK
-    own = pl.BlockSpec((rows, PAIR), lambda p: (0, p))
-    wide = pl.BlockSpec((ext, PAIR), lambda p: (0, p))
-    both = lambda n: pl.BlockSpec((2, n, PAIR), lambda p: (0, 0, p))
+    halo_first, halo_pairs = halo
+    before = () if before is None else tuple(before)
+    own = pl.BlockSpec((rows, PAIR), lambda p: (0, p + first))
+    wide = pl.BlockSpec((ext, PAIR), lambda p: (0, p + first))
+    edge = pl.BlockSpec((2, reach, PAIR), lambda p: (0, 0, p + first - halo_first))
     return pl.pallas_call(
         functools.partial(attend_back_kernel, chunk),
         grid=(pairs,),
@@ -302,15 +302,22 @@
             wide,
             own,
             own,
-            pl.BlockSpec((1, 2, rows), lambda p: (p, 0, 0)),
+            pl.BlockSpec((1, 2, rows), lambda p: (p + first, 0, 0)),
+        ]
+        + [pl.BlockSpec(memory_space=pl.ANY)] * len(before),
+        out_specs=[
+            own,
+            pl.BlockSpec((2, rows, PAIR), lambda p: (0, 0, p + first)),
+            edge,
+            edge,
         ],
-        out_specs=[own, both(rows), both(reach), both(reach)],
         out_shape=[
             shape((rows, width), full),
             shape((2, rows, width), full),
-            shape((2, reach, width), low),
-            shape((2, reach, width), low),
+            shape((2, reach, halo_pairs * PAIR), low),
+            shape((2, reach, halo_pairs * PAIR), low),
         ],
+        input_output_aliases={7 + i: i for i in range(len(before))},
         scratch_shapes=[
             pltpu.VMEM((blocks, span, QUERY_BLOCK), full),
             pltpu.VMEM((PAIR, ext), low),
@@ -318,13 +325,9 @@
             pltpu.VMEM((ext, PAIR), full),
         ],
         compiler_params=params(),
-        cost_estimate=pl.CostEstimate(
-            flops=40 * rows * span * width,
-            bytes_accessed=20 * rows * width,
-            transcendentals=rows * span * width // HEAD,
-        ),
+        cost_estimate=cost(8 * pairs),
         name="attend_back",
-    )(bounds, q, k, v, o, do, lse)
+    )(bounds, q, k, v, o, do, lse, *before)
 
 
 def mean(x):
@@ -363,21 +366,19 @@
         sems,
     ) = refs[sources:]
     step = pl.program_id(0)
-    copies = plan(ids, srcs, (out_w, gate_w, up_w, down_w), sems)
+    weights = (out_w, gate_w, up_w, down_w)
 
     @pl.when(step == 0)
     def _():
-        for group in copies:
-            for copy in group:
-                copy.start()
+        for copy in plan(ids, srcs, weights, sems):
+            copy.start()
         gains_ref[...] = jnp.zeros_like(gains_ref)
 
-    def ready(*groups):
+    def ready(*which):
         @pl.when(step == 0)
         def _():
-            for group in groups:
-                for copy in copies[group]:
-                    copy.wait()
+            for i in which:
+                pltpu.make_async_copy(weights[i], weights[i], sems.at[i]).wait()
 
     parts, _, width = gate_w.shape
     gain1, bias1, gain2, bias2 = (vec_ref[i : i + 1] for i in range(4))
@@ -472,11 +473,7 @@
             shape((8, width), full),
         ],
         compiler_params=params(),
-        cost_estimate=pl.CostEstimate(
-            flops=2 * rows * width * (2 * width + 6 * hidden),
-            bytes_accessed=40 << 20,
-            transcendentals=rows * hidden,
-        ),
+        cost_estimate=cost(53),
         name="middle",
     )(ids, attended, tokens, cot, vectors, *sources)
 
@@ -498,115 +495,98 @@
         out_specs=pl.BlockSpec((tile_a, tile_b), lambda i, j: (i, j)),
         out_shape=shape((size_a, size_b), low),
         compiler_params=params(),
-        cost_estimate=pl.CostEstimate(
-            flops=2 * rows * size_a * size_b,
-            bytes_accessed=2 * (rows * (size_a + size_b) + size_a * size_b),
-            transcendentals=0,
-        ),
+        cost_estimate=cost(9),
         name="weight_grad",
     )(a, b)
 
 
-def joint_kernel(reach, dq_ref, own_ref, prior_ref, next_ref, cos_ref, sin_ref, dj_ref):
+def joint_kernel(halos, dq_ref, own_ref, *refs):
+    priors = refs[:halos]
+    nexts = refs[halos : 2 * halos]
+    cos_ref, sin_ref, dj_ref = refs[2 * halos :]
     block, width = dq_ref.shape
-    step = pl.program_id(0)
-    early = step < pl.num_programs(0) // 2
+    early = pl.program_id(0) < pl.num_programs(0) // 2
     cosine = cos_ref[...]
     sine = sin_ref[...]
-    for at in range(0, width, PAIR):
-        lanes = slice(at, at + PAIR)
-        near = [
-            jnp.where(early, prior_ref[i, :, lanes], next_ref[i, :, lanes]).astype(full)
-            for i in range(2)
-        ]
-        dj_ref[:, lanes] = turn_back(dq_ref[:, lanes], cosine, sine).astype(low)
-        dj_ref[:, width + at : width + at + PAIR] = turn_back(
-            own_ref[0, :, lanes] + near[0], cosine, sine
-        ).astype(low)
-        dj_ref[:, 2 * width + at : 2 * width + at + PAIR] = (
-            own_ref[1, :, lanes] + near[1]
-        ).astype(low)
-
-
-def joint(dq, own, prior, following, cosine, sine):
+    start = 0
+    for prior_ref, next_ref in zip(priors, nexts):
+        for at in range(0, prior_ref.shape[2], PAIR):
+            near = [
+                jnp.where(
+                    early, prior_ref[i, :, at : at + PAIR], next_ref[i, :, at : at + PAIR]
+                ).astype(full)
+                for i in range(2)
+            ]
+            lanes = slice(start + at, start + at + PAIR)
+            keys = turn_back(own_ref[0, :, lanes] + near[0], cosine, sine)
+            dj_ref[0, :, lanes] = turn_back(dq_ref[:, lanes], cosine, sine).astype(low)
+            dj_ref[1, :, lanes] = keys.astype(low)
+            dj_ref[2, :, lanes] = (own_ref[1, :, lanes] + near[1]).astype(low)
+        start += prior_ref.shape[2]
+
+
+def joint(dq, own, priors, nexts, cosine, sine):
     rows, width = dq.shape
-    reach = prior.shape[1]
     block = TOKEN_BLOCK
-    half = reach // block
-    tile = lambda w: pl.BlockSpec((block, w), lambda i: (i, 0))
+    half = priors[0].shape[1] // block
     inner = pl.BlockSpec((block, PAIR), lambda i: (i + half, 0))
+    edges = [
+        pl.BlockSpec((2, block, p.shape[2]), lambda i: (0, jnp.minimum(i, half - 1), 0))
+        for p in priors
+    ] + [
+        pl.BlockSpec((2, block, p.shape[2]), lambda i: (0, jnp.maximum(i - half, 0), 0))
+        for p in nexts
+    ]
     return pl.pallas_call(
-        functools.partial(joint_kernel, reach),
+        functools.partial(joint_kernel, len(priors)),
         grid=(rows // block,),
         in_specs=[
-            tile(width),
+            pl.BlockSpec((block, width), lambda i: (i, 0)),
             pl.BlockSpec((2, block, width), lambda i: (0, i, 0)),
-            pl.BlockSpec((2, block, width), lambda i: (0, jnp.minimum(i, half - 1), 0)),
-            pl.BlockSpec((2, block, width), lambda i: (0, jnp.maximum(i - half, 0), 0)),
-            inner,
-            inner,
-        ],
-        out_specs=tile(3 * width),
-        out_shape=shape((rows, 3 * width), low),
+        ]
+        + edges
+        + [inner, inner],
+        out_specs=pl.BlockSpec((3, block, width), lambda i: (0, i, 0)),
+        out_shape=shape((3, rows, width), low),
         compiler_params=params(),
-        cost_estimate=pl.CostEstimate(
-            flops=12 * rows * width, bytes_accessed=24 * rows * width, transcendentals=0
-        ),
+        cost_estimate=cost(9),
         name="joint",
-    )(dq, own, prior, following, cosine, sine)
-
-
-def input_grad_kernel(plan, sources, ids, dj_ref, dz1_ref, *refs):
-    srcs = refs[:sources]
-    out_ref, weight, sems = refs[sources:]
-    copies = plan(ids, srcs, weight, sems)
-
-    @pl.when(pl.program_id(0) == 0)
-    def _():
-        for copy in copies:
-            copy.start()
-        for copy in copies:
-            copy.wait()
-
-    width = dz1_ref.shape[1]
+    )(dq, own, *priors, *nexts, cosine, sine)
+
+
+def input_grad_kernel(dj_ref, dz1_ref, weight_ref, out_ref):
     out = dz1_ref[...]
     for i in range(3):
-        out = out + dot_nt(dj_ref[:, i * width : (i + 1) * width], weight[i])
+        out = out + dot_nt(dj_ref[i], weight_ref[i])
     out_ref[...] = out
 
 
-def input_grad(plan, ids, dj, dz1, sources):
+def input_grad(dj, dz1, weights):
     rows, width = dz1.shape
     block = TOKEN_BLOCK
-    tile = lambda w: pl.BlockSpec((block, w), lambda i, *_: (i, 0))
+    tile = pl.BlockSpec((block, width), lambda i: (i, 0))
     return pl.pallas_call(
-        functools.partial(input_grad_kernel, plan, len(sources)),
-        grid_spec=pltpu.PrefetchScalarGridSpec(
-            num_scalar_prefetch=1,
-            grid=(rows // block,),
-            in_specs=[tile(3 * width), tile(width)]
-            + [pl.BlockSpec(memory_space=pl.ANY)] * len(sources),
-            out_specs=tile(width),
-            scratch_shapes=[
-                pltpu.VMEM((3, width, width), low),
-                pltpu.SemaphoreType.DMA((1,)),
-            ],
-        ),
+        input_grad_kernel,
+        grid=(rows // block,),
+        in_specs=[
+            pl.BlockSpec((3, block, width), lambda i: (0, i, 0)),
+            tile,
+            pl.BlockSpec((3, width, width), lambda i: (0, 0, 0)),
+        ],
+        out_specs=tile,
         out_shape=shape((rows, width), full),
         compiler_params=params(),
-        cost_estimate=pl.CostEstimate(
-            flops=6 * rows * width * width, bytes_accessed=14 * rows * width, transcendentals=0
-        ),
+        cost_estimate=cost(10),
         name="input_grad",
-    )(ids, dj, dz1, *sources)
-
-
-def whole_joint_plan(ids, srcs, weight, sems):
+    )(dj, dz1, weights)
+
+
+def whole_joint_plan(ids, srcs, weight, sem):
     width = weight.shape[1]
     return [
-        pltpu.make_async_copy(srcs[0].at[:, i * width : (i + 1) * width], weight.at[i], sems.at[0])
+        pltpu.make_async_copy(srcs[0].at[:, i * width : (i + 1) * width], weight.at[i], sem)
         for i in range(3)
-    ]
+    ] + [pltpu.make_async_copy(srcs[1], weight.at[3], sem)]
 
 
 def whole_middle_plan(ids, srcs, weights, sems):
@@ -616,15 +596,224 @@
         pltpu.make_async_copy(src.at[:, i * width : (i + 1) * width], dst.at[i], sem)
         for i in range(parts)
     ]
-    return [
-        [pltpu.make_async_copy(srcs[0], out_w, sems.at[0])],
-        columns(srcs[1], gate_w, sems.at[1]),
-        columns(srcs[2], up_w, sems.at[2]),
-        [pltpu.make_async_copy(srcs[3], down_w, sems.at[3])],
-    ]
+    return (
+        [pltpu.make_async_copy(srcs[0].at[3], out_w, sems.at[0])]
+        + columns(srcs[1], gate_w, sems.at[1])
+        + columns(srcs[2], up_w, sems.at[2])
+        + [pltpu.make_async_copy(srcs[3], down_w, sems.at[3])]
+    )
+
+
+def swap_with(value, place):
+    pairs = []
+    for r in range(4):
+        for z in range(4):
+            for c in range(2):
+                to_r, to_z, to_c = place(r, z, c)
+                pairs.append(((r * 4 + z) * 2 + c, (to_r * 4 + to_z) * 2 + to_c))
+    return lax.ppermute(value, ("rep", "fsdp"), pairs)
+
+
+def over_core(value):
+    return swap_with(value, lambda r, z, c: (r, z, 1 - c))
+
+
+def over_z(value, k):
+    return swap_with(value, lambda r, z, c: (r, z ^ k, c))
+
+
+def over_square_1(value):
+    return swap_with(value, lambda r, z, c: (r ^ (1 + c), z, c))
+
+
+def over_square_2(value):
+    return swap_with(value, lambda r, z, c: (r ^ (2 - c), z, c))
+
+
+def pieces(ids, srcs):
+    r, z, c = ids[0], ids[1], ids[2]
+    found = []
+    for core, (shard, near, far) in ((c, srcs[:3]), (1 - c, srcs[3:6])):
+        bit1, bit2 = 1 + core, 2 - core
+        for quarter in range(4):
+            found.append((shard.at[quarter], quarter, z, core))
+        for ref, base in ((near, r), (far, r ^ bit2)):
+            for j in range(2):
+                for k in range(1, 4):
+                    found.append((ref.at[j, k - 1], base ^ bit1 if j else base, z ^ k, core))
+    return found
+
+
+def piece_joint_plan(ids, srcs, weight, sem):
+    size = srcs[0].shape[1]
+    copies = []
+    for ref, quarter, z, core in pieces(ids, srcs):
+        at = pl.multiple_of((2 * z + core) * size, size)
+        copies.append(pltpu.make_async_copy(ref, weight.at[quarter, pl.ds(at, size)], sem))
+    return copies
+
+
+def piece_middle_plan(ids, srcs, weights, sems):
+    out_w, gate_w, up_w, down_w = weights
+    size = srcs[1].shape[1] // 3
+    copies = [pltpu.make_async_copy(srcs[0].at[3], out_w, sems.at[0])]
+    found = pieces(ids, srcs[1:])
+    for i, target in enumerate((gate_w, up_w)):
+        for ref, quarter, z, core in found:
+            at = pl.multiple_of((2 * z + core) * size, size)
+            copies.append(
+                pltpu.make_async_copy(
+                    ref.at[i * size : (i + 1) * size],
+                    target.at[quarter, pl.ds(at, size)],
+                    sems.at[1 + i],
+                )
+            )
+    for ref, quarter, z, core in found:
+        at = pl.multiple_of(((2 * z + core) * 4 + quarter) * size, size)
+        copies.append(
+            pltpu.make_async_copy(
+                ref.at[2 * size : 3 * size], down_w.at[pl.ds(at, size)], sems.at[3]
+            )
+        )
+    return copies
+
+
+def gather_quarters(shard, mine, extra):
+    n, width = shard.shape[1:]
+    arrived = [over_z(mine, k) for k in (1, 2, 3)]
+    mate_shard = over_core(shard)
+    own = jnp.stack([a[:n] for a in arrived])
+    other = over_square_1(own)
+    near = jnp.stack([own, other])
+    far = over_square_2(near)
+    mate_near = over_core(near)
+    mate_far = over_core(far)
+    return [shard, near, far, mate_shard, mate_near, mate_far], arrived
+
+
+def flip(value, axis, bit):
+    return jnp.where(bit == 1, jnp.flip(value, axis), value)
+
+
+def position(j, core):
+    return jnp.where(core == 0, j, (j & 1) * 2 + (j >> 1))
+
+
+def put_pieces(ids, block_ref, own_ref, other_ref, first, size):
+    z, c = ids[1], ids[2]
+    for ref, core in ((own_ref, c), (other_ref, 1 - c)):
+        for k in range(4):
+            at = pl.multiple_of((2 * (z ^ k) + core) * size, 8)
+            ref[0, k, first : first + size, :] = block_ref[pl.ds(at, size), :].astype(low)
+
+
+def gate_up_grad_kernel(ids, hidden_ref, dgate_ref, dlift_ref, gains_ref, own_ref, other_ref, block_ref):
+    size = block_ref.shape[0] // 8
+    z, c = ids[1], ids[2]
+    quarter = ids[0] ^ pl.program_id(0)
+    for i, ref in enumerate((dgate_ref, dlift_ref)):
+        block_ref[...] = dot_tn(hidden_ref[...], ref[...])
+        put_pieces(ids, block_ref, own_ref, other_ref, i * size, size)
+    for ref, core in ((own_ref, c), (other_ref, 1 - c)):
+        for k in range(4):
+            ref[0, k, 2 * size :, :] = jnp.zeros((16, ref.shape[3]), low)
+            row = gains_ref[quarter * 8 + 2 * (z ^ k) + core]
+            ref[0, k, 2 * size :, : row.shape[1]] = row.astype(low)
+
+
+def grad_specs(size, width):
+    own = pl.BlockSpec((1, 4, size, width), lambda j, ids: (position(j, ids[2]), 0, 0, 0))
+    other = pl.BlockSpec((1, 4, size, width), lambda j, ids: (position(j, 1 - ids[2]), 0, 0, 0))
+    return [own, other], [shape((4, 4, size, width), low)] * 2
+
+
+def gate_up_grad(ids, hidden_low, dgate, dlift, gains):
+    rows, width = hidden_low.shape
+    size = width // 8
+    out_specs, out_shape = grad_specs(2 * size + 16, width)
+    column = pl.BlockSpec((rows, width), lambda j, ids: (0, ids[0] ^ j))
+    return pl.pallas_call(
+        gate_up_grad_kernel,
+        grid_spec=pltpu.PrefetchScalarGridSpec(
+            num_scalar_prefetch=1,
+            grid=(4,),
+            in_specs=[
+                pl.BlockSpec((rows, width), lambda j, ids: (0, 0)),
+                column,
+                column,
+                pl.BlockSpec(gains.shape, lambda j, ids: (0, 0, 0)),
+            ],
+            out_specs=out_specs,
+            scratch_shapes=[pltpu.VMEM((width, width), full)],
+        ),
+        out_shape=out_shape,
+        compiler_params=params(),
+        cost_estimate=cost(18),
+        name="gate_up_grad",
+    )(ids, hidden_low, dgate, dlift, gains)
+
+
+def joint_grad_kernel(ids, tok_ref, dj_ref, at_ref, db_ref, own_ref, other_ref, block_ref):
+    size = block_ref.shape[0] // 8
+    quarter = ids[0] ^ pl.program_id(0)
+
+    @pl.when(quarter < 3)
+    def _():
+        block_ref[...] = dot_tn(tok_ref[...], dj_ref[0])
+
+    @pl.when(quarter == 3)
+    def _():
+        block_ref[...] = dot_tn(at_ref[...], db_ref[...])
+
+    put_pieces(ids, block_ref, own_ref, other_ref, 0, size)
+
+
+def joint_grad(ids, tokens, djoint, attended, dbranch):
+    rows, width = tokens.shape
+    size = width // 8
+    out_specs, out_shape = grad_specs(size, width)
+    whole = pl.BlockSpec((rows, width), lambda j, ids: (0, 0))
+    return pl.pallas_call(
+        joint_grad_kernel,
+        grid_spec=pltpu.PrefetchScalarGridSpec(
+            num_scalar_prefetch=1,
+            grid=(4,),
+            in_specs=[
+                whole,
+                pl.BlockSpec(
+                    (1, rows, width), lambda j, ids: (jnp.minimum(ids[0] ^ j, 2), 0, 0)
+                ),
+                whole,
+                whole,
+            ],
+            out_specs=out_specs,
+            scratch_shapes=[pltpu.VMEM((width, width), full)],
+        ),
+        out_shape=out_shape,
+        compiler_params=params(),
+        cost_estimate=cost(9),
+        name="joint_grad",
+    )(ids, tokens, djoint, attended, dbranch)
+
+
+def reduce_pieces(own, other, r, c):
+    wide = lambda v: v.astype(full)
+    a = over_core(other)
+    b = over_square_2((wide(own[2:]) + wide(a[2:])).astype(low))
+    d = over_square_1((wide(own[1]) + wide(a[1]) + wide(b[1])).astype(low))
+    kept = wide(own[0]) + wide(a[0]) + wide(b[0]) + wide(d)
+    e = over_z(kept[2:].astype(low), 2)
+    f = over_z((kept[1] + wide(e[1])).astype(low), 1)
+    mine = (kept[0] + wide(e[0]) + wide(f)).astype(low)
+    pair = jnp.stack([mine, over_square_1(mine)])
+    four = jnp.stack([pair, over_square_2(pair)])
+    four = jnp.where(c == 1, jnp.swapaxes(four, 0, 1), four)
+    four = flip(flip(four, 1, r & 1), 0, r >> 1)
+    return four.reshape(4, *mine.shape).astype(full)
 
 
 def shards(
+    custom,
     tokens,
     lengths,
     qkv_weight,
@@ -644,6 +833,23 @@
     me = lax.axis_index("fsdp")
     up = [(i, i + 1) for i in range(size - 1)]
     down = [(i + 1, i) for i in range(size - 1)]
+    r = lax.axis_index("rep")
+    z, c = me // 2, me % 2
+    ids = jnp.stack([r, z, c]).astype(jnp.int32)
+    vectors = jnp.stack([norm1_gain, norm1_bias, norm2_gain, norm2_bias]).astype(low)
+
+    if custom:
+        part = qkv_weight.shape[0]
+        columns = lambda w: jnp.swapaxes(w.astype(low).reshape(part, -1, width), 0, 1)
+        first_shard = jnp.concatenate([columns(qkv_weight), out_weight.astype(low)[None]])
+        mine = lax.dynamic_index_in_dim(first_shard, r, 0, keepdims=False)
+        joint_sources, arrived = gather_quarters(first_shard, mine, 0)
+        joint_plan = piece_joint_plan
+    else:
+        gather = lambda w: lax.all_gather(w.astype(low), "fsdp", axis=0, tiled=True)
+        joint_sources = [gather(qkv_weight), gather(out_weight)]
+        joint_plan = whole_joint_plan
+
     tokens_ext = jnp.concatenate(
         [
             lax.ppermute(tokens[rows - REACH :], "fsdp", up),
@@ -652,6 +858,32 @@
         ],
         axis=0,
     )
+
+    if custom:
+        second_shard = jnp.concatenate(
+            [
+                columns(gate_weight),
+                columns(up_weight),
+                down_weight.astype(low).reshape(4, part, width),
+            ],
+            axis=1,
+        )
+        second_shard = lax.optimization_barrier((second_shard, *arrived))[0]
+        rows_of = jnp.pad(vectors, ((0, 12), (0, width - part)))
+        mine = jnp.concatenate(
+            [lax.dynamic_index_in_dim(second_shard, r, 0, keepdims=False), rows_of]
+        )
+        middle_sources, arrived = gather_quarters(second_shard, mine, 16)
+        found = jnp.stack([rows_of] + [a[3 * part :] for a in arrived])
+        found = jnp.stack([found, over_core(found)])[:, :, :4, :part].reshape(2, 2, 2, 4, part)
+        found = flip(flip(flip(found, 0, c), 1, z >> 1), 2, z & 1)
+        vectors = jnp.transpose(found, (3, 1, 2, 0, 4)).reshape(4, width)
+        middle_plan = piece_middle_plan
+    else:
+        middle_sources = [gather(w) for w in (gate_weight, up_weight, down_weight)]
+        vectors = lax.all_gather(vectors, "fsdp", axis=1, tiled=True)
+        middle_plan = whole_middle_plan
+    vectors = jnp.concatenate([vectors, vectors], axis=0).astype(full)
 
     doc_lengths = lengths[0]
     ends = jnp.cumsum(doc_lengths)
@@ -672,43 +904,73 @@
         ]
     ).astype(jnp.int32)
 
-    ids = jnp.zeros((8,), jnp.int32)
-    gather = lambda w: lax.all_gather(w.astype(low), "fsdp", axis=0, tiled=True)
-    qkv_full = gather(qkv_weight)
-    weights = [gather(w) for w in (out_weight, gate_weight, up_weight, down_weight)]
-    vectors = jnp.stack([norm1_gain, norm1_bias, norm2_gain, norm2_bias])
-    vectors = lax.all_gather(vectors.astype(low), "fsdp", axis=1, tiled=True).astype(full)
-    vectors = jnp.concatenate([vectors, vectors], axis=0)
-
-    queries, keys, values = project(
-        whole_joint_plan, ids, tokens_ext, cosine, sine, [qkv_full], rows
+    queries, keys, values, joint_weights = project(
+        joint_plan, ids, tokens_ext, cosine, sine, joint_sources, rows
     )
-    attended, lse = attend(bounds, queries, keys, values)
+    done = None
+    for first in (0, 2, 4):
+        done = attend(bounds, queries, keys, values, first, 2, done)
+    attended, lse = done
     result, dz1, dattended, hidden_low, product, dfeed, dgate, dlift, dbranch, gains = middle(
-        whole_middle_plan, ids, attended, tokens, cotangent, vectors, weights, hidden
+        middle_plan,
+        ids,
+        attended,
+        tokens,
+        cotangent,
+        vectors,
+        [joint_weights, *middle_sources],
+        hidden,
     )
+    gains = gains[:4]
     spread = lambda g: lax.psum_scatter(g, "fsdp", scatter_dimension=0, tiled=True)
     share_down = spread(weight_grad(product, dfeed))
-    share_gate = spread(weight_grad(hidden_low, dgate))
-    share_up = spread(weight_grad(hidden_low, dlift))
-    share_out = spread(weight_grad(attended, dbranch))
-    share_gains = lax.psum_scatter(gains[:4], "fsdp", scatter_dimension=1, tiled=True)
-
-    dq, dkv, to_prior, to_next = attend_back(
-        bounds, queries, keys, values, attended, dattended, lse
-    )
-    from_prior = lax.ppermute(to_next, "fsdp", up)
-    from_next = lax.ppermute(to_prior, "fsdp", down)
+    if custom:
+        gains = jnp.pad(gains.reshape(32, 1, part), ((0, 0), (0, 15), (0, PAIR - part)))
+        gate_up = gate_up_grad(ids, hidden_low, dgate, dlift, gains)
+    else:
+        share_gate = spread(weight_grad(hidden_low, dgate))
+        share_up = spread(weight_grad(hidden_low, dlift))
+        share_out = spread(weight_grad(attended, dbranch))
+        share_gains = lax.psum_scatter(gains, "fsdp", scatter_dimension=1, tiled=True)
+
+    given = (bounds, queries, keys, values, attended, dattended, lse)
+    done = attend_back(*given, 0, 2, (0, 4))
+    dq, dkv, to_prior, to_next = attend_back(*given, 2, 2, (0, 4), done)
+    from_prior = [lax.ppermute(to_next, "fsdp", up)]
+    from_next = [lax.ppermute(to_prior, "fsdp", down)]
+    dq, dkv, to_prior, to_next = attend_back(*given, 4, 2, (4, 2), (dq, dkv))
+    from_prior.append(lax.ppermute(to_next, "fsdp", up))
+    from_next.append(lax.ppermute(to_prior, "fsdp", down))
     djoint = joint(dq, dkv, from_prior, from_next, cosine, sine)
-    share_qkv = spread(weight_grad(tokens, djoint))
-    grad_tokens = input_grad(whole_joint_plan, ids, djoint, dz1, [qkv_full])
-    summed = lax.psum(
-        tuple(
-            s.astype(full)
-            for s in (share_qkv, share_out, share_gate, share_up, share_down, share_gains)
-        ),
-        "rep",
-    )
+    if custom:
+        joint_pieces = joint_grad(ids, tokens, djoint, attended, dbranch)
+    else:
+        share_qkv = jnp.concatenate([spread(weight_grad(tokens, djoint[i])) for i in range(3)], 1)
+    grad_tokens = input_grad(djoint, dz1, joint_weights)
+
+    if custom:
+        down_sum = share_down
+        for over in (over_square_1, over_square_2):
+            down_sum = (down_sum.astype(full) + over(down_sum).astype(full)).astype(low)
+        natural = lambda v: jnp.swapaxes(v, 0, 1).reshape(part, -1)
+        gate_up = reduce_pieces(*gate_up, r, c)
+        joint_sum = reduce_pieces(*joint_pieces, r, c)
+        summed = (
+            natural(joint_sum[:3]),
+            joint_sum[3],
+            natural(gate_up[:, :part]),
+            natural(gate_up[:, part : 2 * part]),
+            down_sum.astype(full),
+            gate_up[:, 2 * part, :part],
+        )
+    else:
+        summed = lax.psum(
+            tuple(
+                s.astype(full)
+                for s in (share_qkv, share_out, share_gate, share_up, share_down, share_gains)
+            ),
+            "rep",
+        )
     return (result, grad_tokens, *summed[:5], *(summed[5][i] for i in range(4)))
 
 
@@ -716,8 +978,9 @@
     rows = P(("rep", "fsdp"), None)
     matrix = P("fsdp", None)
     vector = P("fsdp")
+    custom = (mesh.shape["rep"], mesh.shape["fsdp"]) == (4, 8)
     return jax.shard_map(
-        shards,
+        functools.partial(shards, custom and not FORCE_WHOLE),
         mesh=mesh,
         in_specs=(rows, P("rep", None)) + (matrix,) * 5 + (vector,) * 4 + (rows,),
         out_specs=(rows, rows) + (matrix,) * 5 + (vector,) * 4,

time: 780 us -> 521 us (0.67)
  blocking collectives: 202 us -> 0 us
  waiting for transfers between devices: 311 us -> 168 us
  starting transfers between devices: 7.67 us -> 51.2 us
  other arithmetic: 16.8 us -> 35.2 us
  local copies, waits for them, and re-layouts: 6.14 us -> 18.3 us
  Pallas kernels: 211 us -> 223 us
    reduce_scatter x5 -> x1, waiting for transfers between devices: 188 us -> 0.02 us  [shards(): lax.psum_scatter(g, 'fsdp', scatter_dimension=0, tiled=True)]
    ppermute x2 -> x37, waiting for transfers between devices: 4.21 us -> 168 us  [the longest x33 168 us: swap_with(): return lax.ppermute(value, ('rep', 'fsdp'), pairs)]
    psum x1 -> x0, blocking collectives: 159 us -> none  [shards(): lax.psum(tuple((s.astype(full) for s in (share_qkv, share_out, share_gate...]
    all_gather x5 -> x0, waiting for transfers between devices: 119 us -> none  [shards(): gather = lambda w: lax.all_gather(w.astype(low), 'fsdp', axis=0, tiled=True)]
    ppermute x2 -> x37, starting transfers between devices: 3.53 us -> 47.7 us  [the longest x33 40.1 us: swap_with(): return lax.ppermute(value, ('rep', 'fsdp'), pairs)]
    all_gather x1 -> x0, blocking collectives: 43 us -> none  [shards(): lax.all_gather(vectors.astype(low), 'fsdp', axis=1, tiled=True).astype(full)]
    pallas_call x5 -> x1, Pallas kernels: 40 us -> 9.46 us  [weight_grad(): pl.pallas_call(weight_grad_kernel, grid=(size_a // tile_a, size_b // tile...]
    pallas_call x2 -> x4, Pallas kernels: 19.4 us -> 45.8 us  [the longest x1 16 us: gate_up_grad(): pl.pallas_call(gate_up_grad_kernel, grid_spec=pltpu.PrefetchScalarGridSpe...]
  transfers between devices with their start and end apart: 15 -> 40, of which waited for: 9 -> 16; matrix products, arithmetic and copies ran while one was open for 2% -> 8% of each run, Pallas kernels for 20% -> 30%
where the time goes in v2:
time: 521 us; the launch traced here: 511 us
  Pallas kernels  223 us (43%)
  waiting for transfers between devices  168 us (32%)
  starting transfers between devices  51.2 us (10%)
  other arithmetic  35.2 us (7%)
  local copies, waits for them, and re-layouts  18.3 us (4%)
  between operations  15.4 us (3%)
    ppermute x33, waiting for transfers between devices, swap_with(): return lax.ppermute(value, ('rep', 'fsdp'), pairs)  168 us
    pallas_call x3, Pallas kernels, attend_back(): pl.pallas_call(functools.partial(attend_back_kernel, chunk), grid=(pairs,...  54.4 us
    pallas_call x1, Pallas kernels, middle(): pl.pallas_call(functools.partial(middle_kernel, plan, len(sources)), grid...  53.6 us
    pallas_call x3, Pallas kernels, attend(): pl.pallas_call(functools.partial(attend_kernel, chunk), grid=(pairs,), in...  42.1 us
    ppermute x33, starting transfers between devices, swap_with(): return lax.ppermute(value, ('rep', 'fsdp'), pairs)  40.1 us
    pallas_call x1, Pallas kernels, project(): pl.pallas_call(functools.partial(project_kernel, plan, len(sources), firs...  17.3 us
    pallas_call x1, Pallas kernels, gate_up_grad(): pl.pallas_call(gate_up_grad_kernel, grid_spec=pltpu.PrefetchScalarGridSpe...  16 us
    pallas_call x1, Pallas kernels, joint_grad(): pl.pallas_call(joint_grad_kernel, grid_spec=pltpu.PrefetchScalarGridSpec(...  11.3 us
  transfers between devices with their start and end apart: 40, of which 16 were waited for; matrix products, arithmetic and copies ran while one was open for 8% of the time, Pallas kernels for 30%

profile of v2, /device:TPU:0, one launch (start us, length us, event | category | flops | bytes accessed | tf_op | source)
XLA Modules:
  0.0 511.1 jit_solution(11352001428281877626)
XLA Ops:
  8.8 3.1 collective-permute-start.2
  11.9 2.6 collective-permute-start.3
  15.7 2.2 collective-permute-start
  21.8 5.5 %fusion.1 = (f32[2048,128]{1,0:T(8,128)}, f32[2048,128]{1,0:T(8,128)}) fusion(f32[128]{0:T(128)S(1)} %get-tuple-element.107, f32[128]{0:T(128)S(1)} %get-tuple-element.108, f32[2048]{0:T(1024)S(1)} %subtract_convert_fusion), kind=kLoop, calls=%fused_computation.23 | loop fusion | flops 524288 | bytes 2106368 | tf_op jit(solution)/shard_map/mul | solution.py:58
  27.6 6.0 %collective-permute-start.12 = (bf16[304,768]{1,0:T(8,128)(2,1)S(1)}, bf16[304,768]{1,0:T(8,128)(2,1)S(1)}, u32[]{:S(2)}, u32[]{:S(2)}) collective-permute-start(bf16[304,768]{1,0:T(8,128)(2,1)S(1)} %pad_maximum_fusion.9), channel_id=1, source_target_pairs={{0,6},{1,7},{2,4},{3,5},{4,2},{5,3},{6,0},{7,1},{8,14},{9,15},{10,... | collective-permute-start | bytes 1400840 | tf_op jit(solution)/shard_map/ppermute | solution.py:614
  34.4 2.1 fusion.37
  36.5 10.0 %collective-permute-done.12 = bf16[304,768]{1,0:T(8,128)(2,1)S(1)} collective-permute-done((bf16[304,768]{1,0:T(8,128)(2,1)S(1)}, bf16[304,768]{1,0:T(8,128)(2,1)S(1)}, u32[]{:S(2)}, u32[]{:S(2)}) %collective-permute-start.12) | collective-permute-done | bytes 466976 | tf_op jit(solution)/shard_map/ppermute | solution.py:614
  48.0 28.1 %collective-permute-done.11 = bf16[304,768]{1,0:T(8,128)(2,1)S(1)} collective-permute-done((bf16[304,768]{1,0:T(8,128)(2,1)S(1)}, bf16[304,768]{1,0:T(8,128)(2,1)S(1)}, u32[]{:S(2)}, u32[]{:S(2)}) %collective-permute-start.11) | collective-permute-done | bytes 466976 | tf_op jit(solution)/shard_map/ppermute | solution.py:614
  81.1 2.1 pad_maximum_fusion.5.refs_1_
  88.6 13.7 %collective-permute-done.6.refs_2_ = bf16[2,3,96,768]{3,2,1,0:T(8,128)(2,1)} collective-permute-done((bf16[2,3,96,768]{3,2,1,0:T(8,128)(2,1)}, bf16[2,3,96,768]{3,2,1,0:T(8,128)(2,1)}, u32[]{:S(2)}, u32[]{:S(2)}) %collective-permute-start.6) | collective-permute-done | bytes 884768 | tf_op jit(solution)/shard_map/ppermute | solution.py:614
  102.6 3.1 collective-permute-done.14
  105.7 3.1 pad_maximum_fusion.1.refs_2_
  111.7 2.9 pad_maximum_fusion.tok_ref
  114.7 17.3 %project.1 = (bf16[1024,768]{1,0:T(8,128)(2,1)}, bf16[2048,768]{1,0:T(8,128)(2,1)}, bf16[2048,768]{1,0:T(8,128)(2,1)}, bf16[4,768,768]{2,1,0:T(8,128)(2,1)}) custom-call(s32[3]{0:T(128)} %pad_add_fusion.1.ids, bf16[2048,768]{1,0:T(8,128)(2,1)} %pad_maximum_fusion.tok_ref, f32[2048,128]{1,0:T(8,128)} %get-tuple-element.104.cos_ref.refs_4_, ...), custom_call_target="tpu_custom_call" | custom-call | flops 17250000896 | bytes 1048576 | tf_op jit(solution)/shard_map/project/pallas_call | solution.py:109
  132.0 9.2 %collective-permute-done.15.refs_3_ = bf16[2,3,288,768]{3,2,1,0:T(8,128)(2,1)} collective-permute-done((bf16[2,3,288,768]{3,2,1,0:T(8,128)(2,1)}, bf16[2,3,288,768]{3,2,1,0:T(8,128)(2,1)}, u32[]{:S(2)}, u32[]{:S(2)}) %collective-permute-start.15) | collective-permute-done | bytes 2654240 | tf_op jit(solution)/shard_map/ppermute | solution.py:614
  141.1 14.1 %attend.3 = (bf16[1024,768]{1,0:T(8,128)(2,1)}, f32[6,2,1024]{2,1,0:T(2,128)}) custom-call(s32[2,1024]{1,0:T(2,128)} %pad_add_fusion.bounds_ref, bf16[1024,768]{1,0:T(8,128)(2,1)} %get-tuple-element.48.q_ref, bf16[2048,768]{1,0:T(8,128)(2,1)} %get-tuple-element.49.k_ref, bf16[2048,768]{1,0:T(8,128)(2,1)} %get-tuple-element.50.v_ref), custom_call_target="tpu_custom_call" | custom-call | flops 13799999488 | bytes 1048576 | tf_op jit(solution)/shard_map/attend/pallas_call | solution.py:200
  155.2 14.1 %attend.4 = (bf16[1024,768]{1,0:T(8,128)(2,1)}, f32[6,2,1024]{2,1,0:T(2,128)}) custom-call(s32[2,1024]{1,0:T(2,128)} %pad_add_fusion.bounds_ref, bf16[1024,768]{1,0:T(8,128)(2,1)} %get-tuple-element.48.q_ref, bf16[2048,768]{1,0:T(8,128)(2,1)} %get-tuple-element.49.k_ref, ...), custom_call_target="tpu_custom_call", output_to_operand_aliasing={{0}: (4, {}), {1}: (5, {})} | custom-call | flops 13799999488 | bytes 1048576 | tf_op jit(solution)/shard_map/attend/pallas_call | solution.py:200
  169.3 13.9 %attend.5 = (bf16[1024,768]{1,0:T(8,128)(2,1)}, f32[6,2,1024]{2,1,0:T(2,128)}) custom-call(s32[2,1024]{1,0:T(2,128)} %pad_add_fusion.bounds_ref, bf16[1024,768]{1,0:T(8,128)(2,1)} %get-tuple-element.48.q_ref, bf16[2048,768]{1,0:T(8,128)(2,1)} %get-tuple-element.49.k_ref, ...), custom_call_target="tpu_custom_call", output_to_operand_aliasing={{0}: (4, {}), {1}: (5, {})} | custom-call | flops 13799999488 | bytes 1048576 | tf_op jit(solution)/shard_map/attend/pallas_call | solution.py:200
  186.3 53.6 %middle.1 = (bf16[1024,768]{1,0:T(8,128)(2,1)}, f32[1024,768]{1,0:T(8,128)}, bf16[1024,768]{1,0:T(8,128)(2,1)}, bf16[1024,768]{1,0:T(8,128)(2,1)}, bf16[1024,307...) custom-call(s32[3]{0:T(128)} %pad_add_fusion.1.ids, ...), custom_call_target="tpu_custom_call" | custom-call | flops 60949999616 | bytes 1048576 | tf_op jit(solution)/shard_map/middle/pallas_call | solution.py:434
  241.4 16.0 %gate_up_grad.1 = (bf16[4,4,208,768]{3,2,1,0:T(8,128)(2,1)}, bf16[4,4,208,768]{3,2,1,0:T(8,128)(2,1)}) custom-call(s32[3]{0:T(128)} %pad_add_fusion.1.ids, bf16[1024,768]{1,0:T(8,128)(2,1)} %get-tuple-element.77.hidden_ref, bf16[1024,3072]{1,0:T(8,128)(2,1)} %get-tuple-element.78.dgate_ref, bf16[1024,3072]{1,0:T(8,128)(2,1)} %get-tuple-element.79.dlift_ref, ...), custom_call_target="tpu_custom_call" | custom-call | flops 20700000256 | bytes 1048576 | tf_op jit(solution)/shard_map/gate_up_grad/pallas_call | solution.py:735
  257.9 18.1 %attend_back.3 = (f32[1024,768]{1,0:T(8,128)}, f32[2,1024,768]{2,1,0:T(8,128)}, bf16[2,512,512]{2,1,0:T(8,128)(2,1)}, bf16[2,512,512]{2,1,0:T(8,128)(2,1)}) custom-call(s32[2,1024]{1,0:T(2,128)} %pad_add_fusion.bounds_ref, bf16[1024,768]{1,0:T(8,128)(2,1)} %get-tuple-element.48.q_ref, bf16[2048,768]{1,0:T(8,128)(2,1)} %get-tuple-element.49.k_ref, ...), custom_call_target="tpu_custom_call" | custom-call | flops 18400000000 | bytes 1048576 | tf_op jit(solution)/shard_map/attend_back/pallas_call | solution.py:295
  276.0 18.1 %attend_back.4 = (f32[1024,768]{1,0:T(8,128)}, f32[2,1024,768]{2,1,0:T(8,128)}, bf16[2,512,512]{2,1,0:T(8,128)(2,1)}, bf16[2,512,512]{2,1,0:T(8,128)(2,1)}) custom-call(s32[2,1024]{1,0:T(2,128)} %pad_add_fusion.bounds_ref, bf16[1024,768]{1,0:T(8,128)(2,1)} %get-tuple-element.48.q_ref, ...), custom_call_target="tpu_custom_call", output_to_operand_aliasing={{0}: (7, {}), {1}: (8, {}), {2}: (9, {}), {3}: (10, {})} | custom-call | flops 18400000000 | bytes 1048576 | tf_op jit(solution)/shard_map/attend_back/pallas_call | solution.py:295
  294.2 2.0 collective-permute-start.19
  297.4 18.2 %attend_back.5 = (f32[1024,768]{1,0:T(8,128)}, f32[2,1024,768]{2,1,0:T(8,128)}, bf16[2,512,256]{2,1,0:T(8,128)(2,1)}, bf16[2,512,256]{2,1,0:T(8,128)(2,1)}) custom-call(s32[2,1024]{1,0:T(2,128)} %pad_add_fusion.bounds_ref, bf16[1024,768]{1,0:T(8,128)(2,1)} %get-tuple-element.48.q_ref, ...), custom_call_target="tpu_custom_call", output_to_operand_aliasing={{0}: (7, {}), {1}: (8, {})} | custom-call | flops 18400000000 | bytes 1048576 | tf_op jit(solution)/shard_map/attend_back/pallas_call | solution.py:295
  315.6 3.1 collective-permute-start.20
  320.0 9.5 %weight_grad.1 = bf16[3072,768]{1,0:T(8,128)(2,1)} custom-call(bf16[1024,3072]{1,0:T(8,128)(2,1)} %get-tuple-element.83.a_ref, bf16[1024,768]{1,0:T(8,128)(2,1)} %get-tuple-element.84.b_ref), custom_call_target="tpu_custom_call" | custom-call | flops 10350000128 | bytes 1048576 | tf_op jit(solution)/shard_map/weight_grad/pallas_call | solution.py:488
  331.2 9.4 %joint.1.dj_ref = bf16[3,1024,768]{2,1,0:T(8,128)(2,1)} custom-call(f32[1024,768]{1,0:T(8,128)} %get-tuple-element.67.dq_ref, f32[2,1024,768]{2,1,0:T(8,128)} %get-tuple-element.68.own_ref, bf16[2,512,512]{2,1,0:T(8,128)(2,1)} %copy-done.21, bf16[2,512,256]{2,1,0:T(8,128)(2,1)} %copy-done.23, bf16[2,512,512]{2,1,0:T(8,128)(2,1)} %copy-done.22, ...), custom_call_target="tpu_custom_call" | custom-call | flops 10350000128 | bytes 1048576 | tf_op jit(solution)/shard_map/joint/pallas_call | solution.py:540
  340.5 11.3 %joint_grad.1 = (bf16[4,4,96,768]{3,2,1,0:T(8,128)(2,1)}, bf16[4,4,96,768]{3,2,1,0:T(8,128)(2,1)}) custom-call(s32[3]{0:T(128)} %pad_add_fusion.1.ids, bf16[1024,768]{1,0:T(8,128)(2,1)} %tok_ref.3, bf16[3,1024,768]{2,1,0:T(8,128)(2,1)} %joint.1.dj_ref, bf16[1024,768]{1,0:T(8,128)(2,1)} %get-tuple-element.55.at_ref.o_ref, ...), custom_call_target="tpu_custom_call" | custom-call | flops 10350000128 | bytes 1048576 | tf_op jit(solution)/shard_map/joint_grad/pallas_call | solution.py:776
  351.9 1.8 collective-permute-start.23
  353.7 2.5 add_convert_fusion
  358.4 1.6 collective-permute-start.24
  360.0 39.9 %collective-permute-done.24 = bf16[2,4,96,768]{3,2,1,0:T(8,128)(2,1)S(1)} collective-permute-done((bf16[2,4,96,768]{3,2,1,0:T(8,128)(2,1)S(1)}, bf16[2,4,96,768]{3,2,1,0:T(8,128)(2,1)S(1)}, u32[]{:S(2)}, u32[]{:S(2)}) %collective-permute-start.24) | collective-permute-done | bytes 1179680 | tf_op jit(solution)/shard_map/ppermute | solution.py:614
  401.7 2.7 fusion
  405.0 5.0 collective-permute-done.25
  411.8 13.2 %collective-permute-done.26 = bf16[2,96,768]{2,1,0:T(8,128)(2,1)S(1)} collective-permute-done((bf16[2,96,768]{2,1,0:T(8,128)(2,1)S(1)}, bf16[2,96,768]{2,1,0:T(8,128)(2,1)S(1)}, u32[]{:S(2)}, u32[]{:S(2)}) %collective-permute-start.26) | collective-permute-done | bytes 294944 | tf_op jit(solution)/shard_map/ppermute | solution.py:614
  425.0 5.1 %collective-permute-done.27 = bf16[96,768]{1,0:T(8,128)(2,1)S(1)} collective-permute-done((bf16[96,768]{1,0:T(8,128)(2,1)S(1)}, bf16[96,768]{1,0:T(8,128)(2,1)S(1)}, u32[]{:S(2)}, u32[]{:S(2)}) %collective-permute-start.27) | collective-permute-done | bytes 147488 | tf_op jit(solution)/shard_map/ppermute | solution.py:614
  431.8 4.9 collective-permute-done.28
  436.8 1.7 collective-permute-start.29
  438.4 3.0 bitcast_add_fusion
  442.4 9.1 %input_grad.1 = f32[1024,768]{1,0:T(8,128)} custom-call(bf16[3,1024,768]{2,1,0:T(8,128)(2,1)} %joint.1.dj_ref, f32[1024,768]{1,0:T(8,128)} %get-tuple-element.73.dz1_ref, bf16[4,768,768]{2,1,0:T(8,128)(2,1)} %get-tuple-element.57.refs_0_.weight_ref), custom_call_target="tpu_custom_call" | custom-call | flops 11500000256 | bytes 1048576 | tf_op jit(solution)/shard_map/input_grad/pallas_call | solution.py:568
  451.6 16.1 %collective-permute-done.33 = bf16[2,208,768]{2,1,0:T(8,128)(2,1)S(1)} collective-permute-done((bf16[2,208,768]{2,1,0:T(8,128)(2,1)S(1)}, bf16[2,208,768]{2,1,0:T(8,128)(2,1)S(1)}, u32[]{:S(2)}, u32[]{:S(2)}) %collective-permute-start.33) | collective-permute-done | bytes 639008 | tf_op jit(solution)/shard_map/ppermute | solution.py:614
  469.1 1.8 collective-permute-start.37
  471.0 6.5 %collective-permute-done.34 = bf16[208,768]{1,0:T(8,128)(2,1)} collective-permute-done((bf16[208,768]{1,0:T(8,128)(2,1)S(1)}, bf16[208,768]{1,0:T(8,128)(2,1)}, u32[]{:S(2)}, u32[]{:S(2)}) %collective-permute-start.34) | collective-permute-done | bytes 319520 | tf_op jit(solution)/shard_map/ppermute | solution.py:614
  478.6 1.8 collective-permute-start.35
  480.7 1.6 collective-permute-start.38
  482.4 6.7 %collective-permute-done.35 = bf16[208,768]{1,0:T(8,128)(2,1)S(1)} collective-permute-done((bf16[208,768]{1,0:T(8,128)(2,1)S(1)}, bf16[208,768]{1,0:T(8,128)(2,1)S(1)}, u32[]{:S(2)}, u32[]{:S(2)}) %collective-permute-start.35) | collective-permute-done | bytes 319520 | tf_op jit(solution)/shard_map/ppermute | solution.py:614
  489.2 1.7 collective-permute-start.36
  493.8 5.8 %collective-permute-done.36 = bf16[2,208,768]{2,1,0:T(8,128)(2,1)S(1)} collective-permute-done((bf16[2,208,768]{2,1,0:T(8,128)(2,1)S(1)}, bf16[2,208,768]{2,1,0:T(8,128)(2,1)S(1)}, u32[]{:S(2)}, u32[]{:S(2)}) %collective-permute-start.36) | collective-permute-done | bytes 639008 | tf_op jit(solution)/shard_map/ppermute | solution.py:614
  (184 shorter events, 50.7 us)
Async XLA Ops:
  7.2 7.3 %copy-start = (bf16[1024,768]{1,0:T(8,128)(2,1)S(1)}, bf16[1024,768]{1,0:T(8,128)(2,1)}, u32[]{:S(2)}) copy-start(bf16[1024,768]{1,0:T(8,128)(2,1)} %tok_ref.3) | copy-start | bytes 4718596
  7.2 461.8 %reduce-scatter.2.cloned.1.call-start = ((), (), s32[]{:S(2)}) async-start(), calls=%async_computation.1 | async-start | bytes 5308416 | tf_op jit(solution)/shard_map/reduce_scatter | solution.py:925
  8.7 10.5 %copy-start.13 = (s32[1,8]{1,0:T(1,128)S(1)}, s32[1,8]{1,0:T(1,128)}, u32[]{:S(2)}) copy-start(s32[1,8]{1,0:T(1,128)} %param.13) | copy-start | bytes 100
  8.8 10.8 %copy-start.4 = (f32[96,3072]{1,0:T(8,128)S(1)}, f32[96,3072]{1,0:T(8,128)}, u32[]{:S(2)}) copy-start(f32[96,3072]{1,0:T(8,128)} %param.16) | copy-start | bytes 3538948
  8.8 18.7 %collective-permute-start.2 = (bf16[96,768]{1,0:T(8,128)(2,1)S(1)}, bf16[96,768]{1,0:T(8,128)(2,1)}, u32[]{:S(2)}, u32[]{:S(2)}) collective-permute-start(bf16[96,768]{1,0:T(8,128)(2,1)S(1)} %fusion.15), channel_id=1, source_target_pairs={{0,2},{1,3},{2,0},{3,1},{4,6},{5,7},{6,4},{7,5},{8,10},{9,11},{10,... | collective-permute-start | bytes 442376 | tf_op jit(solution)/shard_map/ppermute | solution.py:614
  11.9 15.6 %collective-permute-start.3 = (bf16[96,768]{1,0:T(8,128)(2,1)S(1)}, bf16[96,768]{1,0:T(8,128)(2,1)}, u32[]{:S(2)}, u32[]{:S(2)}) collective-permute-start(bf16[96,768]{1,0:T(8,128)(2,1)S(1)} %fusion.15), channel_id=1, source_target_pairs={{0,4},{1,5},{2,6},{3,7},{4,0},{5,1},{6,2},{7,3},{8,12},{9,13},{10,... | collective-permute-start | bytes 442376 | tf_op jit(solution)/shard_map/ppermute | solution.py:614
  14.4 13.0 %collective-permute-start.4 = (bf16[96,768]{1,0:T(8,128)(2,1)S(1)}, bf16[96,768]{1,0:T(8,128)(2,1)}, u32[]{:S(2)}, u32[]{:S(2)}) collective-permute-start(bf16[96,768]{1,0:T(8,128)(2,1)S(1)} %fusion.15), channel_id=1, source_target_pairs={{0,6},{1,7},{2,4},{3,5},{4,2},{5,3},{6,0},{7,1},{8,14},{9,15},{10,... | collective-permute-start | bytes 442376 | tf_op jit(solution)/shard_map/ppermute | solution.py:614
  15.7 94.7 %collective-permute-start = (bf16[512,768]{1,0:T(8,128)(2,1)}, bf16[512,768]{1,0:T(8,128)(2,1)}, u32[]{:S(2)}, u32[]{:S(2)}) collective-permute-start(bf16[512,768]{1,0:T(8,128)(2,1)} %get-tuple-element.91), channel_id=1, source_target_pairs={{0,1},{1,2},{2,3},{3,4},{4,5},{5,6},{6,7},{8,9},{9,10},{10,11},{11... | collective-permute-start | bytes 2359304 | tf_op jit(solution)/shard_map/ppermute | solution.py:855
  17.9 93.3 %collective-permute-start.1 = (bf16[512,768]{1,0:T(8,128)(2,1)}, bf16[512,768]{1,0:T(8,128)(2,1)}, u32[]{:S(2)}, u32[]{:S(2)}) collective-permute-start(bf16[512,768]{1,0:T(8,128)(2,1)} %get-tuple-element.92), channel_id=1, source_target_pairs={{1,0},{2,1},{3,2},{4,3},{5,4},{6,5},{7,6},{9,8},{10,9},{11,10},{12... | collective-permute-start | bytes 2359304 | tf_op jit(solution)/shard_map/ppermute | solution.py:857
  27.4 20.5 %copy-start.1 = (bf16[4,288,768]{2,1,0:T(8,128)(2,1)}, bf16[4,288,768]{2,1,0:T(8,128)(2,1)S(1)}, u32[]{:S(2)}) copy-start(bf16[4,288,768]{2,1,0:T(8,128)(2,1)S(1)} %pad_maximum_fusion.2.refs_1_) | copy-start | bytes 5308420
  27.6 18.9 %collective-permute-start.12 = (bf16[304,768]{1,0:T(8,128)(2,1)S(1)}, bf16[304,768]{1,0:T(8,128)(2,1)S(1)}, u32[]{:S(2)}, u32[]{:S(2)}) collective-permute-start(bf16[304,768]{1,0:T(8,128)(2,1)S(1)} %pad_maximum_fusion.9), channel_id=1, source_target_pairs={{0,6},{1,7},{2,4},{3,5},{4,2},{5,3},{6,0},{7,1},{8,14},{9,15},{10,... | collective-permute-start | bytes 1400840 | tf_op jit(solution)/shard_map/ppermute | solution.py:614
  33.7 42.4 %collective-permute-start.11 = (bf16[304,768]{1,0:T(8,128)(2,1)S(1)}, bf16[304,768]{1,0:T(8,128)(2,1)S(1)}, u32[]{:S(2)}, u32[]{:S(2)}) collective-permute-start(bf16[304,768]{1,0:T(8,128)(2,1)S(1)} %pad_maximum_fusion.9), channel_id=1, source_target_pairs={{0,4},{1,5},{2,6},{3,7},{4,0},{5,1},{6,2},{7,3},{8,12},{9,13},{10,... | collective-permute-start | bytes 1400840 | tf_op jit(solution)/shard_map/ppermute | solution.py:614
  33.8 42.3 %collective-permute-start.10 = (bf16[304,768]{1,0:T(8,128)(2,1)S(1)}, bf16[304,768]{1,0:T(8,128)(2,1)S(1)}, u32[]{:S(2)}, u32[]{:S(2)}) collective-permute-start(bf16[304,768]{1,0:T(8,128)(2,1)S(1)} %pad_maximum_fusion.9), channel_id=1, source_target_pairs={{0,2},{1,3},{2,0},{3,1},{4,6},{5,7},{6,4},{7,5},{8,10},{9,11},{10,... | collective-permute-start | bytes 1400840 | tf_op jit(solution)/shard_map/ppermute | solution.py:614
  46.4 29.7 %copy-start.9 = (bf16[304,768]{1,0:T(8,128)(2,1)}, bf16[304,768]{1,0:T(8,128)(2,1)S(1)}, u32[]{:S(2)}) copy-start(bf16[304,768]{1,0:T(8,128)(2,1)S(1)} %collective-permute-done.12) | copy-start | bytes 1400836
  46.4 34.7 %collective-permute-start.5 = (bf16[3,96,768]{2,1,0:T(8,128)(2,1)}, bf16[3,96,768]{2,1,0:T(8,128)(2,1)}, u32[]{:S(2)}, u32[]{:S(2)}) collective-permute-start(bf16[3,96,768]{2,1,0:T(8,128)(2,1)} %get-tuple-element.98), channel_id=1, source_target_pairs={{0,8},{1,17},{2,10},{3,19},{4,12},{5,21},{6,14},{7,23},{8,0},{9,25... | collective-permute-start | bytes 1327112 | tf_op jit(solution)/shard_map/ppermute | solution.py:614
  78.1 27.6 %collective-permute-start.14 = (bf16[3,288,768]{2,1,0:T(8,128)(2,1)}, bf16[3,288,768]{2,1,0:T(8,128)(2,1)}, u32[]{:S(2)}, u32[]{:S(2)}) collective-permute-start(bf16[3,288,768]{2,1,0:T(8,128)(2,1)} %get-tuple-element.94), channel_id=1, source_target_pairs={{0,8},{1,17},{2,10},{3,19},{4,12},{5,21},{6,14},{7,23},{8,0},{9,25... | collective-permute-start | bytes 3981320 | tf_op jit(solution)/shard_map/ppermute | solution.py:614
  83.3 19.0 %collective-permute-start.6 = (bf16[2,3,96,768]{3,2,1,0:T(8,128)(2,1)}, bf16[2,3,96,768]{3,2,1,0:T(8,128)(2,1)}, u32[]{:S(2)}, u32[]{:S(2)}) collective-permute-start(bf16[2,3,96,768]{3,2,1,0:T(8,128)(2,1)} %pad_maximum_fusion.5.refs_1_), channel_id=1, source_target_pairs={{0,16},{1,9},{2,18},{3,11},{4,20},{5,13},{6,22},{7,15},{8,24},{9,1... | collective-permute-start | bytes 2654216 | tf_op jit(solution)/shard_map/ppermute | solution.py:614
  87.0 1.4 collective-permute-start.13
  88.4 26.3 %collective-permute-start.8 = (bf16[2,3,96,768]{3,2,1,0:T(8,128)(2,1)}, bf16[2,3,96,768]{3,2,1,0:T(8,128)(2,1)}, u32[]{:S(2)}, u32[]{:S(2)}) collective-permute-start(bf16[2,3,96,768]{3,2,1,0:T(8,128)(2,1)} %pad_maximum_fusion.5.refs_1_), channel_id=1, source_target_pairs={{0,1},{1,0},{2,3},{3,2},{4,5},{5,4},{6,7},{7,6},{8,9},{9,8},{10,11... | collective-permute-start | bytes 2654216 | tf_op jit(solution)/shard_map/ppermute | solution.py:614
  102.3 12.4 %collective-permute-start.9 = (bf16[2,3,96,768]{3,2,1,0:T(8,128)(2,1)}, bf16[2,3,96,768]{3,2,1,0:T(8,128)(2,1)}, u32[]{:S(2)}, u32[]{:S(2)}) collective-permute-start(bf16[2,3,96,768]{3,2,1,0:T(8,128)(2,1)} %collective-permute-done.6.refs_2_), channel_id=1, source_target_pairs={{0,1},{1,0},{2,3},{3,2},{4,5},{5,4},{6,7},{7,6},{8,9},{9,8},{10,11... | collective-permute-start | bytes 2654216 | tf_op jit(solution)/shard_map/ppermute | solution.py:614
  108.8 32.3 %collective-permute-start.15 = (bf16[2,3,288,768]{3,2,1,0:T(8,128)(2,1)}, bf16[2,3,288,768]{3,2,1,0:T(8,128)(2,1)}, u32[]{:S(2)}, u32[]{:S(2)}) collective-permute-start(bf16[2,3,288,768]{3,2,1,0:T(8,128)(2,1)} %pad_maximum_fusion.1.refs_2_), channel_id=1, source_target_pairs={{0,16},{1,9},{2,18},{3,11},{4,20},{5,13},{6,22},{7,15},{8,24},{9,1... | collective-permute-start | bytes 7962632 | tf_op jit(solution)/shard_map/ppermute | solution.py:614
  110.4 4.2 collective-permute-start.7
  111.2 72.1 %collective-permute-start.16 = (bf16[4,288,768]{2,1,0:T(8,128)(2,1)}, bf16[4,288,768]{2,1,0:T(8,128)(2,1)S(1)}, u32[]{:S(2)}, u32[]{:S(2)}) collective-permute-start(bf16[4,288,768]{2,1,0:T(8,128)(2,1)} %copy-done.1), channel_id=1, source_target_pairs={{0,1},{1,0},{2,3},{3,2},{4,5},{5,4},{6,7},{7,6},{8,9},{9,8},{10,11... | collective-permute-start | bytes 5308424 | tf_op jit(solution)/shard_map/ppermute | solution.py:614
  114.6 68.7 %collective-permute-start.17 = (bf16[2,3,288,768]{3,2,1,0:T(8,128)(2,1)}, bf16[2,3,288,768]{3,2,1,0:T(8,128)(2,1)S(1)}, u32[]{:S(2)}, u32[]{:S(2)}) collective-permute-start(bf16[2,3,288,768]{3,2,1,0:T(8,128)(2,1)} %pad_maximum_fusion.1.refs_2_), channel_id=1, source_target_pairs={{0,1},{1,0},{2,3},{3,2},{4,5},{5,4},{6,7},{7,6},{8,9},{9,8},{10,11... | collective-permute-start | bytes 7962632 | tf_op jit(solution)/shard_map/ppermute | solution.py:614
  141.1 42.2 %collective-permute-start.18 = (bf16[2,3,288,768]{3,2,1,0:T(8,128)(2,1)}, bf16[2,3,288,768]{3,2,1,0:T(8,128)(2,1)S(1)}, u32[]{:S(2)}, u32[]{:S(2)}) collective-permute-start(bf16[2,3,288,768]{3,2,1,0:T(8,128)(2,1)} %collective-permute-done.15.refs_3_), channel_id=1, source_target_pairs={{0,1},{1,0},{2,3},{3,2},{4,5},{5,4},{6,7},{7,6},{8,9},{9,8},{10,11... | collective-permute-start | bytes 7962632 | tf_op jit(solution)/shard_map/ppermute | solution.py:614
  257.4 96.3 %collective-permute-start.30 = (bf16[4,4,208,768]{3,2,1,0:T(8,128)(2,1)}, bf16[4,4,208,768]{3,2,1,0:T(8,128)(2,1)}, u32[]{:S(2)}, u32[]{:S(2)}) collective-permute-start(bf16[4,4,208,768]{3,2,1,0:T(8,128)(2,1)} %get-tuple-element.82), channel_id=1, source_target_pairs={{0,1},{1,0},{2,3},{3,2},{4,5},{5,4},{6,7},{7,6},{8,9},{9,8},{10,11... | collective-permute-start | bytes 15335432 | tf_op jit(solution)/shard_map/ppermute | solution.py:614
  294.2 35.4 %collective-permute-start.19 = (bf16[2,512,512]{2,1,0:T(8,128)(2,1)}, bf16[2,512,512]{2,1,0:T(8,128)(2,1)S(1)}, u32[]{:S(2)}, u32[]{:S(2)}) collective-permute-start(bf16[2,512,512]{2,1,0:T(8,128)(2,1)} %get-tuple-element.69), channel_id=1, source_target_pairs={{0,1},{1,2},{2,3},{3,4},{4,5},{5,6},{6,7},{8,9},{9,10},{10,11},{11... | collective-permute-start | bytes 3145736 | tf_op jit(solution)/shard_map/ppermute | solution.py:939
  296.1 33.4 %collective-permute-start.21 = (bf16[2,512,512]{2,1,0:T(8,128)(2,1)}, bf16[2,512,512]{2,1,0:T(8,128)(2,1)S(1)}, u32[]{:S(2)}, u32[]{:S(2)}) collective-permute-start(bf16[2,512,512]{2,1,0:T(8,128)(2,1)} %get-tuple-element.71), channel_id=1, source_target_pairs={{1,0},{2,1},{3,2},{4,3},{5,4},{6,5},{7,6},{9,8},{10,9},{11,10},{12... | collective-permute-start | bytes 3145736 | tf_op jit(solution)/shard_map/ppermute | solution.py:940
  315.6 13.9 %collective-permute-start.20 = (bf16[2,512,256]{2,1,0:T(8,128)(2,1)}, bf16[2,512,256]{2,1,0:T(8,128)(2,1)S(1)}, u32[]{:S(2)}, u32[]{:S(2)}) collective-permute-start(bf16[2,512,256]{2,1,0:T(8,128)(2,1)} %get-tuple-element.70), channel_id=1, source_target_pairs={{0,1},{1,2},{2,3},{3,4},{4,5},{5,6},{6,7},{8,9},{9,10},{10,11},{11... | collective-permute-start | bytes 1572872 | tf_op jit(solution)/shard_map/ppermute | solution.py:942
  318.7 10.8 %collective-permute-start.22 = (bf16[2,512,256]{2,1,0:T(8,128)(2,1)}, bf16[2,512,256]{2,1,0:T(8,128)(2,1)S(1)}, u32[]{:S(2)}, u32[]{:S(2)}) collective-permute-start(bf16[2,512,256]{2,1,0:T(8,128)(2,1)} %get-tuple-element.72), channel_id=1, source_target_pairs={{1,0},{2,1},{3,2},{4,3},{5,4},{6,5},{7,6},{9,8},{10,9},{11,10},{12... | collective-permute-start | bytes 1572872 | tf_op jit(solution)/shard_map/ppermute | solution.py:943
  331.2 22.5 %slice-start = ((s8[5111808]{0:T(1024)(128)(4,1)}), s8[4194304]{0:T(1024)(128)(4,1)S(1)}, s32[]{:S(2)}) async-start(s8[5111808]{0:T(1024)(128)(4,1)} %bitcast.135), calls=%async_computation.2 | async-start | bytes 8388608
  340.5 13.2 %slice-start.1 = ((s8[5111808]{0:T(1024)(128)(4,1)}), s8[917504]{0:T(1024)(128)(4,1)S(1)}, s32[]{:S(2)}) async-start(s8[5111808]{0:T(1024)(128)(4,1)} %bitcast.135), calls=%async_computation.3 | async-start | bytes 1835008
  351.9 6.2 %collective-permute-start.23 = (bf16[4,4,96,768]{3,2,1,0:T(8,128)(2,1)}, bf16[4,4,96,768]{3,2,1,0:T(8,128)(2,1)S(1)}, u32[]{:S(2)}, u32[]{:S(2)}) collective-permute-start(bf16[4,4,96,768]{3,2,1,0:T(8,128)(2,1)} %get-tuple-element.76), channel_id=1, source_target_pairs={{0,1},{1,0},{2,3},{3,2},{4,5},{5,4},{6,7},{7,6},{8,9},{9,8},{10,11... | collective-permute-start | bytes 7077896 | tf_op jit(solution)/shard_map/ppermute | solution.py:614
  356.2 45.5 %collective-permute-start.31 = (bf16[2,4,208,768]{3,2,1,0:T(8,128)(2,1)S(1)}, bf16[2,4,208,768]{3,2,1,0:T(8,128)(2,1)S(1)}, u32[]{:S(2)}, u32[]{:S(2)}) collective-permute-start(bf16[2,4,208,768]{3,2,1,0:T(8,128)(2,1)S(1)} %add_convert_fusion), channel_id=1, source_target_pairs={{0,16},{1,9},{2,18},{3,11},{4,20},{5,13},{6,22},{7,15},{8,24},{9,1... | collective-permute-start | bytes 7667720 | tf_op jit(solution)/shard_map/ppermute | solution.py:614
  358.4 41.5 %collective-permute-start.24 = (bf16[2,4,96,768]{3,2,1,0:T(8,128)(2,1)S(1)}, bf16[2,4,96,768]{3,2,1,0:T(8,128)(2,1)S(1)}, u32[]{:S(2)}, u32[]{:S(2)}) collective-permute-start(bf16[2,4,96,768]{3,2,1,0:T(8,128)(2,1)S(1)} %add_convert_fusion.2), channel_id=1, source_target_pairs={{0,16},{1,9},{2,18},{3,11},{4,20},{5,13},{6,22},{7,15},{8,24},{9,1... | collective-permute-start | bytes 3538952 | tf_op jit(solution)/shard_map/ppermute | solution.py:614
  400.1 9.9 %collective-permute-start.25 = (bf16[4,96,768]{2,1,0:T(8,128)(2,1)S(1)}, bf16[4,96,768]{2,1,0:T(8,128)(2,1)S(1)}, u32[]{:S(2)}, u32[]{:S(2)}) collective-permute-start(bf16[4,96,768]{2,1,0:T(8,128)(2,1)S(1)} %fusion.6), channel_id=1, source_target_pairs={{0,8},{1,17},{2,10},{3,19},{4,12},{5,21},{6,14},{7,23},{8,0},{9,25... | collective-permute-start | bytes 1769480 | tf_op jit(solution)/shard_map/ppermute | solution.py:614
  404.5 34.0 %collective-permute-start.32 = (bf16[4,208,768]{2,1,0:T(8,128)(2,1)S(1)}, bf16[4,208,768]{2,1,0:T(8,128)(2,1)}, u32[]{:S(2)}, u32[]{:S(2)}) collective-permute-start(bf16[4,208,768]{2,1,0:T(8,128)(2,1)S(1)} %fusion), channel_id=1, source_target_pairs={{0,8},{1,17},{2,10},{3,19},{4,12},{5,21},{6,14},{7,23},{8,0},{9,25... | collective-permute-start | bytes 3833864 | tf_op jit(solution)/shard_map/ppermute | solution.py:614
  410.4 14.5 %collective-permute-start.26 = (bf16[2,96,768]{2,1,0:T(8,128)(2,1)S(1)}, bf16[2,96,768]{2,1,0:T(8,128)(2,1)S(1)}, u32[]{:S(2)}, u32[]{:S(2)}) collective-permute-start(bf16[2,96,768]{2,1,0:T(8,128)(2,1)S(1)} %slice.297), channel_id=1, source_target_pairs={{0,4},{1,5},{2,6},{3,7},{4,0},{5,1},{6,2},{7,3},{8,12},{9,13},{10,... | collective-permute-start | bytes 884744 | tf_op jit(solution)/shard_map/ppermute | solution.py:614
  425.0 5.2 %collective-permute-start.27 = (bf16[96,768]{1,0:T(8,128)(2,1)S(1)}, bf16[96,768]{1,0:T(8,128)(2,1)S(1)}, u32[]{:S(2)}, u32[]{:S(2)}) collective-permute-start(bf16[96,768]{1,0:T(8,128)(2,1)S(1)} %fusion.13), channel_id=1, source_target_pairs={{0,2},{1,3},{2,0},{3,1},{4,6},{5,7},{6,4},{7,5},{8,10},{9,11},{10,... | collective-permute-start | bytes 442376 | tf_op jit(solution)/shard_map/ppermute | solution.py:614
  430.2 6.5 %collective-permute-start.28 = (bf16[96,768]{1,0:T(8,128)(2,1)S(1)}, bf16[96,768]{1,0:T(8,128)(2,1)S(1)}, u32[]{:S(2)}, u32[]{:S(2)}) collective-permute-start(bf16[96,768]{1,0:T(8,128)(2,1)S(1)} %fusion.12), channel_id=1, source_target_pairs={{0,8},{1,17},{2,10},{3,19},{4,12},{5,21},{6,14},{7,23},{8,0},{9,25... | collective-permute-start | bytes 442376 | tf_op jit(solution)/shard_map/ppermute | solution.py:614
  436.8 14.7 %collective-permute-start.29 = (bf16[2,96,768]{2,1,0:T(8,128)(2,1)S(1)}, bf16[2,96,768]{2,1,0:T(8,128)(2,1)S(1)}, u32[]{:S(2)}, u32[]{:S(2)}) collective-permute-start(bf16[2,96,768]{2,1,0:T(8,128)(2,1)S(1)} %get-tuple-element.100), channel_id=1, source_target_pairs={{0,16},{1,9},{2,18},{3,11},{4,20},{5,13},{6,22},{7,15},{8,24},{9,1... | collective-permute-start | bytes 884744 | tf_op jit(solution)/shard_map/ppermute | solution.py:614
  441.5 26.2 %collective-permute-start.33 = (bf16[2,208,768]{2,1,0:T(8,128)(2,1)S(1)}, bf16[2,208,768]{2,1,0:T(8,128)(2,1)S(1)}, u32[]{:S(2)}, u32[]{:S(2)}) collective-permute-start(bf16[2,208,768]{2,1,0:T(8,128)(2,1)S(1)} %slice.296), channel_id=1, source_target_pairs={{0,4},{1,5},{2,6},{3,7},{4,0},{5,1},{6,2},{7,3},{8,12},{9,13},{10,... | collective-permute-start | bytes 1916936 | tf_op jit(solution)/shard_map/ppermute | solution.py:614
  468.5 8.9 %collective-permute-start.34 = (bf16[208,768]{1,0:T(8,128)(2,1)S(1)}, bf16[208,768]{1,0:T(8,128)(2,1)}, u32[]{:S(2)}, u32[]{:S(2)}) collective-permute-start(bf16[208,768]{1,0:T(8,128)(2,1)S(1)} %fusion.8), channel_id=1, source_target_pairs={{0,2},{1,3},{2,0},{3,1},{4,6},{5,7},{6,4},{7,5},{8,10},{9,11},{10,... | collective-permute-start | bytes 958472 | tf_op jit(solution)/shard_map/ppermute | solution.py:614
  469.1 11.5 %collective-permute-start.37 = (bf16[384,768]{1,0:T(8,128)(2,1)}, bf16[384,768]{1,0:T(8,128)(2,1)S(1)}, u32[]{:S(2)}, u32[]{:S(2)}) collective-permute-start(bf16[384,768]{1,0:T(8,128)(2,1)} %reduce-scatter.2.cloned.1.call-done), channel_id=1, source_target_pairs={{0,8},{1,17},{2,10},{3,19},{4,12},{5,21},{6,14},{7,23},{8,0},{9,25... | collective-permute-start | bytes 1769480 | tf_op jit(solution)/shard_map/ppermute | solution.py:614
  470.9 9.6 %copy-start.8 = (bf16[384,768]{1,0:T(8,128)(2,1)S(1)}, bf16[384,768]{1,0:T(8,128)(2,1)}, u32[]{:S(2)}) copy-start(bf16[384,768]{1,0:T(8,128)(2,1)} %reduce-scatter.2.cloned.1.call-done) | copy-start | bytes 1769476
  478.6 10.5 %collective-permute-start.35 = (bf16[208,768]{1,0:T(8,128)(2,1)S(1)}, bf16[208,768]{1,0:T(8,128)(2,1)S(1)}, u32[]{:S(2)}, u32[]{:S(2)}) collective-permute-start(bf16[208,768]{1,0:T(8,128)(2,1)S(1)} %fusion.5), channel_id=1, source_target_pairs={{0,8},{1,17},{2,10},{3,19},{4,12},{5,21},{6,14},{7,23},{8,0},{9,25... | collective-permute-start | bytes 958472 | tf_op jit(solution)/shard_map/ppermute | solution.py:614
  480.7 12.0 %collective-permute-start.38 = (bf16[384,768]{1,0:T(8,128)(2,1)S(1)}, bf16[384,768]{1,0:T(8,128)(2,1)S(1)}, u32[]{:S(2)}, u32[]{:S(2)}) collective-permute-start(bf16[384,768]{1,0:T(8,128)(2,1)S(1)} %add_convert_fusion.4), channel_id=1, source_target_pairs={{0,16},{1,9},{2,18},{3,11},{4,20},{5,13},{6,22},{7,15},{8,24},{9,1... | collective-permute-start | bytes 1769480 | tf_op jit(solution)/shard_map/ppermute | solution.py:614
  489.2 10.5 %collective-permute-start.36 = (bf16[2,208,768]{2,1,0:T(8,128)(2,1)S(1)}, bf16[2,208,768]{2,1,0:T(8,128)(2,1)S(1)}, u32[]{:S(2)}, u32[]{:S(2)}) collective-permute-start(bf16[2,208,768]{2,1,0:T(8,128)(2,1)S(1)} %get-tuple-element.96), channel_id=1, source_target_pairs={{0,16},{1,9},{2,18},{3,11},{4,20},{5,13},{6,22},{7,15},{8,24},{9,1... | collective-permute-start | bytes 1916936 | tf_op jit(solution)/shard_map/ppermute | solution.py:614
  (19 other events, 27.9 us)
Sparse Core Ops, SparseCore 0:
  329.6 56.0 reduce-scatter.1
